TPU v7x, 512 devices: a whole 4x8x8 slice. The times are simulated.
512 devices in a mesh: blk: 128 (over z, y, core), view: 4 (over x).
Axes of the slice: x: 4, y: 8, z: 8, core: 2. Of those that a mesh axis runs over, the one named last changes fastest.
Arguments:
- estimate: float32 [4096, 64, 128], P('blk'), may hold values from 0.5 to 2
- view_data: float32 [4, 4096, 64, 128], P('view', 'blk'), may hold values from 0.25 to 4
- slot_block: int32 [4, 128], P('view', 'blk'), may hold values from 0 to 127, each once within a row
- offsets: int32 [4, 128], P('view', 'blk'), may hold values from -8 to 8
- taps: float32 [4, 3, 31], P('view'), may hold values from 0.02 to 1
Outputs:
- deconvolved: float32 [4096, 64, 128], P('blk')
Inputs may be any that keep to these rules, and one draw needn't show every extreme that they name: `slot_block`: each view's row names every block once.
All inputs are finite; a program needn't handle non-finite values.
Results may differ from a plain program's by a relative error of at most 0.0001.
Values sent between devices are 32-bit elements; how exact they have to be, the bound alone decides.
A program may use at most 64 MiB of HBM per device.

v0:
```python
import jax
import jax.numpy as jnp
from jax import lax
from jax.sharding import PartitionSpec as P

ITERS = 2
HALF = 15
RIM = 23


HIGHEST = lax.Precision.HIGHEST


def extended_2(value, sides, width):
    for axis, dim in sides:
        size, length = (lax.axis_size(axis), value.shape[dim])
        up = [(i, (i + 1) % size) for i in range(size - 1)]
        down = [(j, i) for i, j in up]
        last = lax.slice_in_dim(value, length - width, length, axis=dim)
        leading = lax.slice_in_dim(value, 0, width, axis=dim)
        before = lax.ppermute(last, axis, up)
        after = lax.ppermute(leading, axis, down)
        value = jnp.concatenate([before, value, after], axis=dim)
    return value


def banded(weights, offsets_table):
    hits = offsets_table[..., None] == jnp.arange(weights.shape[0], dtype=jnp.int32)
    return jnp.sum(jnp.where(hits, weights, jnp.float32(0.0)), axis=-1)


def toeplitz(length):
    index = jnp.arange(length, dtype=jnp.int32)
    return index[None, :] - index[:, None] + HALF


def relay_blocks(block, source_of, blocks_count):
    pieces = block.reshape(blocks_count, -1)
    exchanged = lax.all_to_all(pieces, "blk", split_axis=0, concat_axis=0, tiled=True)
    chosen = jnp.take(exchanged, source_of, axis=0)
    returned = lax.all_to_all(chosen, "blk", split_axis=0, concat_axis=0, tiled=True)
    return returned.reshape(block.shape)


def blur_and_back(blur_x, measured, mat_y, mat_z):
    blur_y = jnp.einsum("xqz,pq->xpz", blur_x, mat_y, precision=HIGHEST)
    blur_z = jnp.einsum("xyq,pq->xyp", blur_y, mat_z, precision=HIGHEST)
    ratios = measured / blur_z
    back_z = jnp.einsum("xyp,pq->xyq", ratios, mat_z, precision=HIGHEST)
    return jnp.einsum("xpz,pq->xqz", back_z, mat_y, precision=HIGHEST)


def per_device(estimate, view_data, slot_block, offsets, taps):
    blocks_count = lax.axis_size("blk")
    view_count = lax.axis_size("view")
    block_rows = estimate.shape[0]
    window_rows = block_rows + 2 * RIM
    kernel = taps[0] / jnp.sum(taps[0], axis=-1, keepdims=True)
    mat_y = banded(kernel[1], toeplitz(estimate.shape[1]))
    mat_z = banded(kernel[2], toeplitz(estimate.shape[2]))
    x_index = jnp.arange(block_rows, dtype=jnp.int32)
    w_index = jnp.arange(window_rows, dtype=jnp.int32)
    shift_table = w_index[None, :] - RIM - offsets[0, 0] - x_index[:, None] + HALF
    mat_x = banded(kernel[0], shift_table)
    listing = lax.all_gather(slot_block, "blk", axis=1, tiled=True)[0]
    slot_ids = jnp.arange(blocks_count, dtype=jnp.int32)
    holder_of = jnp.sum(
        jnp.where(listing[None, :] == slot_ids[:, None], slot_ids[None, :], 0), axis=1
    )
    measured = view_data[0]
    current = estimate
    for iteration in range(ITERS):
        extended = extended_2(current, (("blk", 0),), RIM)
        blur_x = jnp.einsum("xw,wyz->xyz", mat_x, extended, precision=HIGHEST)
        at_holder = relay_blocks(blur_x, listing, blocks_count)
        back_y = relay_blocks(
            blur_and_back(at_holder, measured, mat_y, mat_z), holder_of, blocks_count
        )
        back_w = jnp.einsum("xw,xyz->wyz", mat_x, back_y, precision=HIGHEST)
        rim_rows = jnp.concatenate([back_w[:RIM], back_w[RIM + block_rows :]], axis=0)
        neighbour_rims = extended_2(rim_rows, (("blk", 0),), RIM)
        own_rows = back_w[RIM : RIM + block_rows]
        own_rows = own_rows + jnp.pad(neighbour_rims[:RIM], ((0, block_rows - RIM), (0, 0), (0, 0)))
        own_rows = own_rows + jnp.pad(
            neighbour_rims[3 * RIM :], ((block_rows - RIM, 0), (0, 0), (0, 0))
        )
        summed = lax.psum(own_rows, "view")
        current = current * (summed / view_count)
    return current


def solution(mesh):
    return jax.shard_map(
        per_device,
        mesh=mesh,
        in_specs=(
            P("blk", None, None),
            P("view", "blk", None, None),
            P("view", "blk"),
            P("view", "blk"),
            P("view", None, None),
        ),
        out_specs=P("blk", None, None),
        check_vma=False,
    )
```

profile of v0, /device:TPU:1, one launch (start us, length us, event | category | flops | bytes accessed | tf_op | source)
XLA Modules:
  0.0 563.0 jit_solution(4079558350566502077)
XLA Ops:
  6.5 2.5 fusion.39
  9.0 4.6 collective-permute-start
  13.6 6.4 %collective-permute-start.1 = (f32[23,64,128]{2,1,0:T(8,128)S(1)}, f32[23,64,128]{2,1,0:T(8,128)}, u32[]{:S(2)}, u32[]{:S(2)}) collective-permute-start(f32[23,64,128]{2,1,0:T(8,128)S(1)} %get-tuple-element.13), channel_id=1, source_target_pairs={{4,0},{8,4},{12,8},{16,12},{20,16},{24,20},{28,24},{32,28},{36,32}... | collective-permute-start | bytes 2261000 | tf_op jit(solution)/shard_map/ppermute | solution.py:22
  20.0 0.6 copy.65
  21.6 0.9 collective-permute-done
  22.5 1.6 copy.51
  24.1 2.6 collective-permute-done.1
  26.7 1.6 copy.53
  28.2 1.6 fusion
  29.9 1.6 copy.54
  31.4 17.2 %all-to-all-start = ((f32[128,1,2048]{2,1,0:T(1,128)}), f32[128,1,2048]{2,1,0:T(1,128)S(1)}, u32[]{:S(2)}, u32[]{:S(2)}) async-start(f32[128,1,2048]{2,1,0:T(1,128)} %bitcast.9), calls=%async_computation | async-start | bytes 2097152 | tf_op jit(solution)/shard_map/all_to_all | solution.py:39
  49.3 1.3 dynamic-slice
  50.6 0.6 bitcast_dynamic-update-slice_fusion
  51.2 38.0 %all-reduce.4 = s32[128]{0:T(128)S(1)} all-reduce(s32[128]{0:T(128)S(1)} %bitcast_dynamic-update-slice_fusion), channel_id=1, replica_groups=mesh['blk'=128,'view'=4] {'blk'}, use_global_device_ids=true, to_apply=%add.4 | all-reduce | flops 128 | bytes 1024 | tf_op jit(solution)/shard_map/squeeze | solution.py:65
  89.5 1.0 gather_fusion
  90.7 2.0 copy.56
  92.7 13.3 %all-to-all-start.1 = ((f32[128,1,2048]{2,1,0:T(1,128)}), f32[128,1,2048]{2,1,0:T(1,128)S(1)}, u32[]{:S(2)}, u32[]{:S(2)}) async-start(f32[128,1,2048]{2,1,0:T(1,128)} %copy.56), calls=%async_computation.1 | async-start | bytes 2097152 | tf_op jit(solution)/shard_map/all_to_all | solution.py:41
  106.5 30.3 %all-to-all-done.1 = f32[128,1,2048]{2,1,0:T(1,128)S(1)} async-done(((f32[128,1,2048]{2,1,0:T(1,128)}), f32[128,1,2048]{2,1,0:T(1,128)S(1)}, u32[]{:S(2)}, u32[]{:S(2)}) %all-to-all-start.1) | async-done | bytes 1048608 | tf_op jit(solution)/shard_map/all_to_all | solution.py:41
  136.8 1.0 convolution_bitcast_fusion.1
  137.9 1.0 convolution_divide_fusion.1
  138.9 1.0 fusion.21
  139.9 2.0 fusion.28
  141.9 6.5 %all-to-all-start.2 = ((f32[128,1,2048]{2,1,0:T(1,128)}), f32[128,1,2048]{2,1,0:T(1,128)S(1)}, u32[]{:S(2)}, u32[]{:S(2)}) async-start(f32[128,1,2048]{2,1,0:T(1,128)} %bitcast.16), calls=%async_computation.2 | async-start | bytes 2097152 | tf_op jit(solution)/shard_map/all_to_all | solution.py:39
  148.5 30.7 %all-to-all-done.2 = f32[128,1,2048]{2,1,0:T(1,128)S(1)} async-done(((f32[128,1,2048]{2,1,0:T(1,128)}), f32[128,1,2048]{2,1,0:T(1,128)S(1)}, u32[]{:S(2)}, u32[]{:S(2)}) %all-to-all-start.2) | async-done | bytes 1048608 | tf_op jit(solution)/shard_map/all_to_all | solution.py:39
  179.6 1.0 gather_fusion.1
  180.7 1.1 copy.59
  181.8 37.4 %all_to_all.84 = f32[128,1,2048]{2,1,0:T(1,128)S(1)} all-to-all(f32[128,1,2048]{2,1,0:T(1,128)S(1)} %copy.59), channel_id=1, replica_groups=mesh['blk'=128,'view'=4] {'blk'}, dimensions={0} | all-to-all | bytes 2097152 | tf_op jit(solution)/shard_map/all_to_all | solution.py:41
  219.2 2.7 fusion.16
  222.2 2.2 collective-permute-start.3
  224.6 3.8 collective-permute-start.2
  228.4 7.2 %collective-permute-done.3 = f32[23,64,128]{2,1,0:T(8,128)S(1)} collective-permute-done((f32[23,64,128]{2,1,0:T(8,128)S(1)}, f32[23,64,128]{2,1,0:T(8,128)S(1)}, u32[]{:S(2)}, u32[]{:S(2)}) %collective-permute-start.3) | collective-permute-done | bytes 753696 | tf_op jit(solution)/shard_map/ppermute | solution.py:22
  236.1 0.9 collective-permute-done.2
  236.9 0.4 copy.62
  237.4 1.2 fusion.13
  238.6 53.2 %all-reduce.8.cloned.1.call-done = f32[32,64,128]{2,0,1:T(8,128)} async-done(((f32[32,64,128]{2,0,1:T(8,128)}), f32[32,64,128]{2,0,1:T(8,128)}) %all-reduce.8.cloned.1.call-update) | async-done | bytes 1048592 | tf_op jit(solution)/shard_map/psum | solution.py:87
  291.8 1.9 multiply_multiply_fusion.1
  294.0 4.0 collective-permute-start.5
  298.1 3.0 collective-permute-start.4
  301.1 7.2 %collective-permute-done.5 = f32[23,64,128]{2,1,0:T(8,128)S(1)} collective-permute-done((f32[23,64,128]{2,1,0:T(8,128)S(1)}, f32[23,64,128]{2,1,0:T(8,128)S(1)}, u32[]{:S(2)}, u32[]{:S(2)}) %collective-permute-start.5) | collective-permute-done | bytes 753696 | tf_op jit(solution)/shard_map/ppermute | solution.py:22
  308.3 0.4 copy.69
  308.8 0.9 collective-permute-done.4
  310.1 1.6 fusion.6
  311.8 0.6 copy.70
  312.4 47.3 %all_to_all.85 = f32[128,1,2048]{2,1,0:T(1,128)S(1)} all-to-all(f32[128,1,2048]{2,1,0:T(1,128)S(1)} %bitcast.97), channel_id=1, replica_groups=mesh['blk'=128,'view'=4] {'blk'}, dimensions={0} | all-to-all | bytes 2097152 | tf_op jit(solution)/shard_map/all_to_all | solution.py:39
  360.0 1.0 gather_fusion.2
  361.2 1.1 copy.72
  362.2 37.3 %all_to_all.86 = f32[128,1,2048]{2,1,0:T(1,128)S(1)} all-to-all(f32[128,1,2048]{2,1,0:T(1,128)S(1)} %copy.72), channel_id=1, replica_groups=mesh['blk'=128,'view'=4] {'blk'}, dimensions={0} | all-to-all | bytes 2097152 | tf_op jit(solution)/shard_map/all_to_all | solution.py:41
  399.6 1.0 convolution_bitcast_fusion
  400.6 1.0 convolution_divide_fusion
  401.6 1.0 fusion.18
  402.6 1.0 fusion.24
  403.6 37.3 %all_to_all.87 = f32[128,1,2048]{2,1,0:T(1,128)S(1)} all-to-all(f32[128,1,2048]{2,1,0:T(1,128)S(1)} %bitcast.96), channel_id=1, replica_groups=mesh['blk'=128,'view'=4] {'blk'}, dimensions={0} | all-to-all | bytes 2097152 | tf_op jit(solution)/shard_map/all_to_all | solution.py:39
  441.3 1.0 gather_fusion.3
  442.4 1.1 copy.75
  443.5 37.2 %all_to_all.88 = f32[128,1,2048]{2,1,0:T(1,128)S(1)} all-to-all(f32[128,1,2048]{2,1,0:T(1,128)S(1)} %copy.75), channel_id=1, replica_groups=mesh['blk'=128,'view'=4] {'blk'}, dimensions={0} | all-to-all | bytes 2097152 | tf_op jit(solution)/shard_map/all_to_all | solution.py:41
  480.7 2.7 fusion.14
  483.7 2.2 collective-permute-start.7
  486.0 3.8 collective-permute-start.6
  489.9 7.2 %collective-permute-done.7 = f32[23,64,128]{2,1,0:T(8,128)S(1)} collective-permute-done((f32[23,64,128]{2,1,0:T(8,128)S(1)}, f32[23,64,128]{2,1,0:T(8,128)S(1)}, u32[]{:S(2)}, u32[]{:S(2)}) %collective-permute-start.7) | collective-permute-done | bytes 753696 | tf_op jit(solution)/shard_map/ppermute | solution.py:22
  497.6 0.9 collective-permute-done.6
  498.9 1.2 fusion.12
  500.1 52.8 %all-reduce.10.cloned.1.call-done = f32[32,64,128]{2,0,1:T(8,128)} async-done(((f32[32,64,128]{2,0,1:T(8,128)}), f32[32,64,128]{2,0,1:T(8,128)}) %all-reduce.10.cloned.1.call-update) | async-done | bytes 1048592 | tf_op jit(solution)/shard_map/psum | solution.py:87
  552.9 1.4 multiply_multiply_fusion
  554.3 1.6 copy.81
  (52 shorter events, 6.0 us)
Async XLA Ops:
  6.5 13.4 %copy-start = (f32[32,64,128]{2,1,0:T(8,128)S(1)}, f32[32,64,128]{2,1,0:T(8,128)}, u32[]{:S(2)}) copy-start(f32[32,64,128]{2,1,0:T(8,128)} %param.7) | copy-start | bytes 3145732
  6.5 14.7 %copy-start.1 = (f32[1,3,31]{2,0,1:T(1,128)S(1)}, f32[1,3,31]{2,0,1:T(1,128)}, u32[]{:S(2)}) copy-start(f32[1,3,31]{2,0,1:T(1,128)} %param.11) | copy-start | bytes 1120
  9.0 13.5 %collective-permute-start = (f32[23,64,128]{2,1,0:T(8,128)}, f32[23,64,128]{2,1,0:T(8,128)}, u32[]{:S(2)}, u32[]{:S(2)}) collective-permute-start(f32[23,64,128]{2,1,0:T(8,128)} %get-tuple-element.12), channel_id=1, source_target_pairs={{0,4},{4,8},{8,12},{12,16},{16,20},{20,24},{24,28},{28,32},{32,36}... | collective-permute-start | bytes 2261000 | tf_op jit(solution)/shard_map/ppermute | solution.py:21
  13.6 13.1 %collective-permute-start.1 = (f32[23,64,128]{2,1,0:T(8,128)S(1)}, f32[23,64,128]{2,1,0:T(8,128)}, u32[]{:S(2)}, u32[]{:S(2)}) collective-permute-start(f32[23,64,128]{2,1,0:T(8,128)S(1)} %get-tuple-element.13), channel_id=1, source_target_pairs={{4,0},{8,4},{12,8},{16,12},{20,16},{24,20},{28,24},{32,28},{36,32}... | collective-permute-start | bytes 2261000 | tf_op jit(solution)/shard_map/ppermute | solution.py:22
  31.4 57.7 %all-to-all-start = ((f32[128,1,2048]{2,1,0:T(1,128)}), f32[128,1,2048]{2,1,0:T(1,128)S(1)}, u32[]{:S(2)}, u32[]{:S(2)}) async-start(f32[128,1,2048]{2,1,0:T(1,128)} %bitcast.9), calls=%async_computation | async-start | bytes 2097152 | tf_op jit(solution)/shard_map/all_to_all | solution.py:39
  92.7 45.1 %copy-start.2 = (f32[1,32,64,128]{3,2,1,0:T(8,128)S(1)}, f32[1,32,64,128]{3,2,1,0:T(8,128)}, u32[]{:S(2)}) copy-start(f32[1,32,64,128]{3,2,1,0:T(8,128)} %param.8) | copy-start | bytes 3145732
  92.7 44.1 %all-to-all-start.1 = ((f32[128,1,2048]{2,1,0:T(1,128)}), f32[128,1,2048]{2,1,0:T(1,128)S(1)}, u32[]{:S(2)}, u32[]{:S(2)}) async-start(f32[128,1,2048]{2,1,0:T(1,128)} %copy.56), calls=%async_computation.1 | async-start | bytes 2097152 | tf_op jit(solution)/shard_map/all_to_all | solution.py:41
  141.9 37.4 %all-to-all-start.2 = ((f32[128,1,2048]{2,1,0:T(1,128)}), f32[128,1,2048]{2,1,0:T(1,128)S(1)}, u32[]{:S(2)}, u32[]{:S(2)}) async-start(f32[128,1,2048]{2,1,0:T(1,128)} %bitcast.16), calls=%async_computation.2 | async-start | bytes 2097152 | tf_op jit(solution)/shard_map/all_to_all | solution.py:39
  148.3 143.5 %all-reduce.8.cloned.1.call-start = ((), (), s32[]{:S(2)}) async-start(), calls=%async_computation.8 | async-start | bytes 2097152 | tf_op jit(solution)/shard_map/psum | solution.py:87
  222.2 13.4 %collective-permute-start.3 = (f32[23,64,128]{2,1,0:T(8,128)S(1)}, f32[23,64,128]{2,1,0:T(8,128)S(1)}, u32[]{:S(2)}, u32[]{:S(2)}) collective-permute-start(f32[23,64,128]{2,1,0:T(8,128)S(1)} %copy.63), channel_id=1, source_target_pairs={{4,0},{8,4},{12,8},{16,12},{20,16},{24,20},{28,24},{32,28},{36,32}... | collective-permute-start | bytes 2261000 | tf_op jit(solution)/shard_map/ppermute | solution.py:22
  224.6 12.4 %collective-permute-start.2 = (f32[23,64,128]{2,1,0:T(8,128)S(1)}, f32[23,64,128]{2,1,0:T(8,128)S(1)}, u32[]{:S(2)}, u32[]{:S(2)}) collective-permute-start(f32[23,64,128]{2,1,0:T(8,128)S(1)} %copy.61), channel_id=1, source_target_pairs={{0,4},{4,8},{8,12},{12,16},{16,20},{20,24},{24,28},{28,32},{32,36}... | collective-permute-start | bytes 2261000 | tf_op jit(solution)/shard_map/ppermute | solution.py:21
  238.6 314.3 %all-reduce.10.cloned.1.call-start = ((), (), s32[]{:S(2)}) async-start(), calls=%async_computation.9 | async-start | bytes 2097152 | tf_op jit(solution)/shard_map/psum | solution.py:87
  294.0 14.4 %collective-permute-start.5 = (f32[23,64,128]{2,1,0:T(8,128)S(1)}, f32[23,64,128]{2,1,0:T(8,128)S(1)}, u32[]{:S(2)}, u32[]{:S(2)}) collective-permute-start(f32[23,64,128]{2,1,0:T(8,128)S(1)} %copy.67), channel_id=1, source_target_pairs={{4,0},{8,4},{12,8},{16,12},{20,16},{24,20},{28,24},{32,28},{36,32}... | collective-permute-start | bytes 2261000 | tf_op jit(solution)/shard_map/ppermute | solution.py:22
  298.1 11.6 %collective-permute-start.4 = (f32[23,64,128]{2,1,0:T(8,128)S(1)}, f32[23,64,128]{2,1,0:T(8,128)S(1)}, u32[]{:S(2)}, u32[]{:S(2)}) collective-permute-start(f32[23,64,128]{2,1,0:T(8,128)S(1)} %copy.66), channel_id=1, source_target_pairs={{0,4},{4,8},{8,12},{12,16},{16,20},{20,24},{24,28},{28,32},{32,36}... | collective-permute-start | bytes 2261000 | tf_op jit(solution)/shard_map/ppermute | solution.py:21
  362.2 38.3 %copy-start.3 = (f32[1,32,64,128]{3,2,1,0:T(8,128)S(1)}, f32[1,32,64,128]{3,2,1,0:T(8,128)}, u32[]{:S(2)}) copy-start(f32[1,32,64,128]{3,2,1,0:T(8,128)} %param.8) | copy-start | bytes 3145732
  483.7 13.4 %collective-permute-start.7 = (f32[23,64,128]{2,1,0:T(8,128)S(1)}, f32[23,64,128]{2,1,0:T(8,128)S(1)}, u32[]{:S(2)}, u32[]{:S(2)}) collective-permute-start(f32[23,64,128]{2,1,0:T(8,128)S(1)} %copy.79), channel_id=1, source_target_pairs={{4,0},{8,4},{12,8},{16,12},{20,16},{24,20},{28,24},{32,28},{36,32}... | collective-permute-start | bytes 2261000 | tf_op jit(solution)/shard_map/ppermute | solution.py:22
  486.0 12.4 %collective-permute-start.6 = (f32[23,64,128]{2,1,0:T(8,128)S(1)}, f32[23,64,128]{2,1,0:T(8,128)S(1)}, u32[]{:S(2)}, u32[]{:S(2)}) collective-permute-start(f32[23,64,128]{2,1,0:T(8,128)S(1)} %copy.77), channel_id=1, source_target_pairs={{0,4},{4,8},{8,12},{12,16},{16,20},{20,24},{24,28},{28,32},{32,36}... | collective-permute-start | bytes 2261000 | tf_op jit(solution)/shard_map/ppermute | solution.py:21
Sparse Core Ops, SparseCore 0:
  238.7 53.0 all-reduce.7
  500.2 52.6 all-reduce.9
where the time goes:
time: 572 us; the launch traced here: 563 us
  blocking collectives  234 us (41%)
  waiting for transfers between devices  195 us (34%)
  starting transfers between devices  67.1 us (12%)
  local copies, waits for them, and re-layouts  26.3 us (5%)
  matrix products  17.7 us (3%)
  between operations  15.4 us (3%)
  other arithmetic  7.15 us (1%)
    all_to_all x3, blocking collectives, relay_blocks(): lax.all_to_all(chosen, 'blk', split_axis=0, concat_axis=0, tiled=True)  112 us
    psum x2, waiting for transfers between devices, per_device(): summed = lax.psum(own_rows, 'view')  106 us
    all_to_all x2, blocking collectives, relay_blocks(): lax.all_to_all(pieces, 'blk', split_axis=0, concat_axis=0, tiled=True)  84.7 us
    squeeze x1, blocking collectives, per_device(): listing = lax.all_gather(slot_block, 'blk', axis=1, tiled=True)[0]  38 us
    all_to_all x2, waiting for transfers between devices, relay_blocks(): lax.all_to_all(pieces, 'blk', split_axis=0, concat_axis=0, tiled=True)  30.7 us
    all_to_all x1, waiting for transfers between devices, relay_blocks(): lax.all_to_all(chosen, 'blk', split_axis=0, concat_axis=0, tiled=True)  30.3 us
    ppermute x4, waiting for transfers between devices, extended_2(): after = lax.ppermute(leading, axis, down)  24.3 us
    all_to_all x2, starting transfers between devices, relay_blocks(): lax.all_to_all(pieces, 'blk', split_axis=0, concat_axis=0, tiled=True)  23.7 us
  transfers between devices with their start and end apart: 13, of which 12 were waited for; matrix products, arithmetic and copies ran while one was open for 1% of the time, Pallas kernels for 0%

commit v1 on v0

--- a/solution.py
+++ b/solution.py
@@ -67,15 +67,12 @@
     holder_of = jnp.sum(
         jnp.where(listing[None, :] == slot_ids[:, None], slot_ids[None, :], 0), axis=1
     )
-    measured = view_data[0]
+    measured = relay_blocks(view_data[0], holder_of, blocks_count)
     current = estimate
     for iteration in range(ITERS):
         extended = extended_2(current, (("blk", 0),), RIM)
         blur_x = jnp.einsum("xw,wyz->xyz", mat_x, extended, precision=HIGHEST)
-        at_holder = relay_blocks(blur_x, listing, blocks_count)
-        back_y = relay_blocks(
-            blur_and_back(at_holder, measured, mat_y, mat_z), holder_of, blocks_count
-        )
+        back_y = blur_and_back(blur_x, measured, mat_y, mat_z)
         back_w = jnp.einsum("xw,xyz->wyz", mat_x, back_y, precision=HIGHEST)
         rim_rows = jnp.concatenate([back_w[:RIM], back_w[RIM + block_rows :]], axis=0)
         neighbour_rims = extended_2(rim_rows, (("blk", 0),), RIM)

time: 572 us -> 315 us (0.55); the launches traced: 563 us -> 314 us
  blocking collectives: 234 us -> 37.9 us
  waiting for transfers between devices: 195 us -> 164 us
  starting transfers between devices: 67.1 us -> 56.6 us
  local copies, waits for them, and re-layouts: 26.3 us -> 15.9 us
    all_to_all x5 -> x0, blocking collectives: 197 us -> none  [the longest x3 112 us: relay_blocks(): lax.all_to_all(chosen, 'blk', split_axis=0, concat_axis=0, tiled=True)]
    squeeze x1 -> x0, blocking collectives: 38 us -> none  [per_device(): listing = lax.all_gather(slot_block, 'blk', axis=1, tiled=True)[0]]
    unnamed x0 -> x1, blocking collectives: none -> 37.9 us
    all_to_all x2 -> x1, waiting for transfers between devices: 30.7 us -> 0.01 us  [relay_blocks(): lax.all_to_all(pieces, 'blk', split_axis=0, concat_axis=0, tiled=True)]
    all_to_all x1, waiting for transfers between devices: 30.3 us -> 0.01 us  [relay_blocks(): lax.all_to_all(chosen, 'blk', split_axis=0, concat_axis=0, tiled=True)]
    ppermute x4, waiting for transfers between devices: 3.55 us -> 24 us  [extended_2(): before = lax.ppermute(last, axis, up)]
    psum x2, waiting for transfers between devices: 106 us -> 118 us  [per_device(): summed = lax.psum(own_rows, 'view')]
    all_to_all x2 -> x1, starting transfers between devices: 23.7 us -> 18.4 us  [relay_blocks(): lax.all_to_all(pieces, 'blk', split_axis=0, concat_axis=0, tiled=True)]
  transfers between devices with their start and end apart: 13 -> 12, of which waited for: 12 -> 10; matrix products, arithmetic and copies ran while one was open for 1% -> 4% of each run, Pallas kernels for 0% -> 0%
where the time goes in v1:
time: 315 us; the launch traced here: 314 us
  waiting for transfers between devices  164 us (52%)
  starting transfers between devices  56.6 us (18%)
  blocking collectives  37.9 us (12%)
  matrix products  17.8 us (6%)
  local copies, waits for them, and re-layouts  15.9 us (5%)
  between operations  15.1 us (5%)
  other arithmetic  6.72 us (2%)
    psum x2, waiting for transfers between devices, per_device(): summed = lax.psum(own_rows, 'view')  118 us
    unnamed x1, blocking collectives  37.9 us
    ppermute x4, waiting for transfers between devices, extended_2(): before = lax.ppermute(last, axis, up)  24 us
    ppermute x4, waiting for transfers between devices, extended_2(): after = lax.ppermute(leading, axis, down)  21.7 us
    all_to_all x1, starting transfers between devices, relay_blocks(): lax.all_to_all(pieces, 'blk', split_axis=0, concat_axis=0, tiled=True)  18.4 us
    ppermute x4, starting transfers between devices, extended_2(): before = lax.ppermute(last, axis, up)  15.3 us
    all_to_all x1, starting transfers between devices, relay_blocks(): lax.all_to_all(chosen, 'blk', split_axis=0, concat_axis=0, tiled=True)  12.9 us
    ppermute x4, starting transfers between devices, extended_2(): after = lax.ppermute(leading, axis, down)  9.9 us
  transfers between devices with their start and end apart: 12, of which 10 were waited for; matrix products, arithmetic and copies ran while one was open for 4% of the time, Pallas kernels for 0%

profile of v1, /device:TPU:1, one launch (start us, length us, event | category | flops | bytes accessed | tf_op | source)
XLA Modules:
  0.0 313.9 jit_solution(8991953783320159728)
XLA Ops:
  6.5 18.4 %all-to-all-start = ((f32[128,1,2048]{2,1,0:T(1,128)}), f32[128,1,2048]{2,1,0:T(1,128)S(1)}, u32[]{:S(2)}, u32[]{:S(2)}) async-start(f32[128,1,2048]{2,1,0:T(1,128)} %bitcast.68), calls=%async_computation | async-start | bytes 2097152 | tf_op jit(solution)/shard_map/all_to_all | solution.py:39
  25.6 1.3 dynamic-slice
  26.9 0.7 bitcast_dynamic-update-slice_fusion
  27.6 37.9 %all-reduce.4 = s32[128]{0:T(128)S(1)} all-reduce(s32[128]{0:T(128)S(1)} %bitcast_dynamic-update-slice_fusion), channel_id=1, replica_groups=mesh['blk'=128,'view'=4] {'blk'}, use_global_device_ids=true, to_apply=%add.4 | all-reduce | flops 128 | bytes 1024
  65.6 0.3 copy.88
  66.0 1.0 gather_fusion
  66.9 0.1 bitcast_select_fusion
  67.1 2.0 copy.47
  69.1 12.9 %all-to-all-start.1 = ((f32[128,1,2048]{2,1,0:T(1,128)}), f32[128,1,2048]{2,1,0:T(1,128)S(1)}, u32[]{:S(2)}, u32[]{:S(2)}) async-start(f32[128,1,2048]{2,1,0:T(1,128)} %copy.47), calls=%async_computation.1 | async-start | bytes 2097152 | tf_op jit(solution)/shard_map/all_to_all | solution.py:41
  82.1 1.3 fusion.40
  83.4 3.5 %collective-permute-start = (f32[23,64,128]{2,1,0:T(8,128)}, f32[23,64,128]{2,1,0:T(8,128)}, u32[]{:S(2)}, u32[]{:S(2)}) collective-permute-start(f32[23,64,128]{2,1,0:T(8,128)} %get-tuple-element.11), channel_id=1, source_target_pairs={{0,4},{4,8},{8,12},{12,16},{16,20},{20,24},{24,28},{28,32},{32,36}... | collective-permute-start | bytes 2261000 | tf_op jit(solution)/shard_map/ppermute | solution.py:21
  87.0 2.1 collective-permute-start.1
  89.1 0.6 copy.58
  90.6 0.1 select_reduce_fusion.2
  90.7 0.2 select_reduce_fusion.1
  90.9 0.3 select_reduce_fusion
  91.2 21.3 %collective-permute-done = f32[23,64,128]{2,1,0:T(8,128)} collective-permute-done((f32[23,64,128]{2,1,0:T(8,128)}, f32[23,64,128]{2,1,0:T(8,128)}, u32[]{:S(2)}, u32[]{:S(2)}) %collective-permute-start) | collective-permute-done | bytes 753696 | tf_op jit(solution)/shard_map/ppermute | solution.py:21
  112.6 1.6 copy.48
  114.1 0.3 collective-permute-done.1
  114.4 1.6 copy.50
  115.9 1.6 fusion
  117.6 1.6 convolution_bitcast_fusion.3
  119.2 1.0 convolution_divide_fusion.1
  120.2 1.0 fusion.23
  121.2 1.0 convolution_bitcast_fusion.2
  122.2 2.7 fusion.17
  125.0 0.1 copy.56
  125.2 1.9 collective-permute-start.3
  127.1 0.1 copy.54
  127.3 4.1 %collective-permute-start.2 = (f32[23,64,128]{2,1,0:T(8,128)S(1)}, f32[23,64,128]{2,1,0:T(8,128)S(1)}, u32[]{:S(2)}, u32[]{:S(2)}) collective-permute-start(f32[23,64,128]{2,1,0:T(8,128)S(1)} %copy.54), channel_id=1, source_target_pairs={{0,4},{4,8},{8,12},{12,16},{16,20},{20,24},{24,28},{28,32},{32,36}... | collective-permute-start | bytes 2261000 | tf_op jit(solution)/shard_map/ppermute | solution.py:21
  131.4 7.2 %collective-permute-done.3 = f32[23,64,128]{2,1,0:T(8,128)S(1)} collective-permute-done((f32[23,64,128]{2,1,0:T(8,128)S(1)}, f32[23,64,128]{2,1,0:T(8,128)S(1)}, u32[]{:S(2)}, u32[]{:S(2)}) %collective-permute-start.3) | collective-permute-done | bytes 753696 | tf_op jit(solution)/shard_map/ppermute | solution.py:22
  138.7 0.4 copy.57
  139.1 0.9 collective-permute-done.2
  140.0 0.4 copy.55
  140.4 1.2 fusion.13
  141.7 58.8 %all-reduce.8.cloned.1.call-done = f32[32,64,128]{2,0,1:T(8,128)} async-done(((f32[32,64,128]{2,0,1:T(8,128)}), f32[32,64,128]{2,0,1:T(8,128)}) %all-reduce.8.cloned.1.call-update) | async-done | bytes 1048592 | tf_op jit(solution)/shard_map/psum | solution.py:84
  200.5 1.9 multiply_multiply_fusion.1
  202.4 0.1 fusion.39
  202.5 0.1 copy.60
  202.7 4.0 %collective-permute-start.5 = (f32[23,64,128]{2,1,0:T(8,128)S(1)}, f32[23,64,128]{2,1,0:T(8,128)S(1)}, u32[]{:S(2)}, u32[]{:S(2)}) collective-permute-start(f32[23,64,128]{2,1,0:T(8,128)S(1)} %copy.60), channel_id=1, source_target_pairs={{4,0},{8,4},{12,8},{16,12},{20,16},{24,20},{28,24},{32,28},{36,32}... | collective-permute-start | bytes 2261000 | tf_op jit(solution)/shard_map/ppermute | solution.py:22
  206.6 0.1 copy.59
  206.8 3.2 %collective-permute-start.4 = (f32[23,64,128]{2,1,0:T(8,128)S(1)}, f32[23,64,128]{2,1,0:T(8,128)S(1)}, u32[]{:S(2)}, u32[]{:S(2)}) collective-permute-start(f32[23,64,128]{2,1,0:T(8,128)S(1)} %copy.59), channel_id=1, source_target_pairs={{0,4},{4,8},{8,12},{12,16},{16,20},{20,24},{24,28},{28,32},{32,36}... | collective-permute-start | bytes 2261000 | tf_op jit(solution)/shard_map/ppermute | solution.py:21
  210.0 7.0 %collective-permute-done.5 = f32[23,64,128]{2,1,0:T(8,128)S(1)} collective-permute-done((f32[23,64,128]{2,1,0:T(8,128)S(1)}, f32[23,64,128]{2,1,0:T(8,128)S(1)}, u32[]{:S(2)}, u32[]{:S(2)}) %collective-permute-start.5) | collective-permute-done | bytes 753696 | tf_op jit(solution)/shard_map/ppermute | solution.py:22
  217.0 0.4 copy.62
  217.5 0.9 collective-permute-done.4
  218.4 0.4 copy.61
  218.8 1.6 fusion.6
  220.4 1.6 convolution_bitcast_fusion.1
  222.0 1.0 convolution_divide_fusion
  223.0 1.0 fusion.20
  224.0 1.0 convolution_bitcast_fusion
  225.1 2.7 fusion.14
  227.9 0.1 copy.68
  228.1 1.9 collective-permute-start.7
  230.0 0.1 copy.66
  230.1 4.4 %collective-permute-start.6 = (f32[23,64,128]{2,1,0:T(8,128)S(1)}, f32[23,64,128]{2,1,0:T(8,128)S(1)}, u32[]{:S(2)}, u32[]{:S(2)}) collective-permute-start(f32[23,64,128]{2,1,0:T(8,128)S(1)} %copy.66), channel_id=1, source_target_pairs={{0,4},{4,8},{8,12},{12,16},{16,20},{20,24},{24,28},{28,32},{32,36}... | collective-permute-start | bytes 2261000 | tf_op jit(solution)/shard_map/ppermute | solution.py:21
  234.5 7.2 %collective-permute-done.7 = f32[23,64,128]{2,1,0:T(8,128)S(1)} collective-permute-done((f32[23,64,128]{2,1,0:T(8,128)S(1)}, f32[23,64,128]{2,1,0:T(8,128)S(1)}, u32[]{:S(2)}, u32[]{:S(2)}) %collective-permute-start.7) | collective-permute-done | bytes 753696 | tf_op jit(solution)/shard_map/ppermute | solution.py:22
  241.8 0.4 copy.69
  242.2 0.9 collective-permute-done.6
  243.1 0.4 copy.67
  243.5 1.2 fusion.12
  244.7 59.3 %all-reduce.10.cloned.1.call-done = f32[32,64,128]{2,0,1:T(8,128)} async-done(((f32[32,64,128]{2,0,1:T(8,128)}), f32[32,64,128]{2,0,1:T(8,128)}) %all-reduce.10.cloned.1.call-update) | async-done | bytes 1048592 | tf_op jit(solution)/shard_map/psum | solution.py:84
  304.1 1.4 multiply_multiply_fusion
  305.5 1.6 copy.70
  (24 shorter events, 0.7 us)
Async XLA Ops:
  6.5 59.1 %all-to-all-start = ((f32[128,1,2048]{2,1,0:T(1,128)}), f32[128,1,2048]{2,1,0:T(1,128)S(1)}, u32[]{:S(2)}, u32[]{:S(2)}) async-start(f32[128,1,2048]{2,1,0:T(1,128)} %bitcast.68), calls=%async_computation | async-start | bytes 2097152 | tf_op jit(solution)/shard_map/all_to_all | solution.py:39
  67.1 15.0 %copy-start = (f32[32,64,128]{2,1,0:T(8,128)S(1)}, f32[32,64,128]{2,1,0:T(8,128)}, u32[]{:S(2)}) copy-start(f32[32,64,128]{2,1,0:T(8,128)} %param.5) | copy-start | bytes 3145732
  69.1 50.0 %all-to-all-start.1 = ((f32[128,1,2048]{2,1,0:T(1,128)}), f32[128,1,2048]{2,1,0:T(1,128)S(1)}, u32[]{:S(2)}, u32[]{:S(2)}) async-start(f32[128,1,2048]{2,1,0:T(1,128)} %copy.47), calls=%async_computation.1 | async-start | bytes 2097152 | tf_op jit(solution)/shard_map/all_to_all | solution.py:41
  82.1 8.3 %copy-start.1 = (f32[1,3,31]{2,0,1:T(1,128)S(1)}, f32[1,3,31]{2,0,1:T(1,128)}, u32[]{:S(2)}) copy-start(f32[1,3,31]{2,0,1:T(1,128)} %param.9) | copy-start | bytes 1120
  82.1 118.5 %all-reduce.8.cloned.1.call-start = ((), (), s32[]{:S(2)}) async-start(), calls=%async_computation.2 | async-start | bytes 2097152 | tf_op jit(solution)/shard_map/psum | solution.py:84
  83.4 29.1 %collective-permute-start = (f32[23,64,128]{2,1,0:T(8,128)}, f32[23,64,128]{2,1,0:T(8,128)}, u32[]{:S(2)}, u32[]{:S(2)}) collective-permute-start(f32[23,64,128]{2,1,0:T(8,128)} %get-tuple-element.11), channel_id=1, source_target_pairs={{0,4},{4,8},{8,12},{12,16},{16,20},{20,24},{24,28},{28,32},{32,36}... | collective-permute-start | bytes 2261000 | tf_op jit(solution)/shard_map/ppermute | solution.py:21
  87.0 27.4 %collective-permute-start.1 = (f32[23,64,128]{2,1,0:T(8,128)}, f32[23,64,128]{2,1,0:T(8,128)}, u32[]{:S(2)}, u32[]{:S(2)}) collective-permute-start(f32[23,64,128]{2,1,0:T(8,128)} %get-tuple-element.12), channel_id=1, source_target_pairs={{4,0},{8,4},{12,8},{16,12},{20,16},{24,20},{28,24},{32,28},{36,32}... | collective-permute-start | bytes 2261000 | tf_op jit(solution)/shard_map/ppermute | solution.py:22
  125.2 13.5 %collective-permute-start.3 = (f32[23,64,128]{2,1,0:T(8,128)S(1)}, f32[23,64,128]{2,1,0:T(8,128)S(1)}, u32[]{:S(2)}, u32[]{:S(2)}) collective-permute-start(f32[23,64,128]{2,1,0:T(8,128)S(1)} %copy.56), channel_id=1, source_target_pairs={{4,0},{8,4},{12,8},{16,12},{20,16},{24,20},{28,24},{32,28},{36,32}... | collective-permute-start | bytes 2261000 | tf_op jit(solution)/shard_map/ppermute | solution.py:22
  127.3 12.7 %collective-permute-start.2 = (f32[23,64,128]{2,1,0:T(8,128)S(1)}, f32[23,64,128]{2,1,0:T(8,128)S(1)}, u32[]{:S(2)}, u32[]{:S(2)}) collective-permute-start(f32[23,64,128]{2,1,0:T(8,128)S(1)} %copy.54), channel_id=1, source_target_pairs={{0,4},{4,8},{8,12},{12,16},{16,20},{20,24},{24,28},{28,32},{32,36}... | collective-permute-start | bytes 2261000 | tf_op jit(solution)/shard_map/ppermute | solution.py:21
  141.6 162.4 %all-reduce.10.cloned.1.call-start = ((), (), s32[]{:S(2)}) async-start(), calls=%async_computation.3 | async-start | bytes 2097152 | tf_op jit(solution)/shard_map/psum | solution.py:84
  202.7 14.4 %collective-permute-start.5 = (f32[23,64,128]{2,1,0:T(8,128)S(1)}, f32[23,64,128]{2,1,0:T(8,128)S(1)}, u32[]{:S(2)}, u32[]{:S(2)}) collective-permute-start(f32[23,64,128]{2,1,0:T(8,128)S(1)} %copy.60), channel_id=1, source_target_pairs={{4,0},{8,4},{12,8},{16,12},{20,16},{24,20},{28,24},{32,28},{36,32}... | collective-permute-start | bytes 2261000 | tf_op jit(solution)/shard_map/ppermute | solution.py:22
  206.8 11.6 %collective-permute-start.4 = (f32[23,64,128]{2,1,0:T(8,128)S(1)}, f32[23,64,128]{2,1,0:T(8,128)S(1)}, u32[]{:S(2)}, u32[]{:S(2)}) collective-permute-start(f32[23,64,128]{2,1,0:T(8,128)S(1)} %copy.59), channel_id=1, source_target_pairs={{0,4},{4,8},{8,12},{12,16},{16,20},{20,24},{24,28},{28,32},{32,36}... | collective-permute-start | bytes 2261000 | tf_op jit(solution)/shard_map/ppermute | solution.py:21
  228.1 13.7 %collective-permute-start.7 = (f32[23,64,128]{2,1,0:T(8,128)S(1)}, f32[23,64,128]{2,1,0:T(8,128)S(1)}, u32[]{:S(2)}, u32[]{:S(2)}) collective-permute-start(f32[23,64,128]{2,1,0:T(8,128)S(1)} %copy.68), channel_id=1, source_target_pairs={{4,0},{8,4},{12,8},{16,12},{20,16},{24,20},{28,24},{32,28},{36,32}... | collective-permute-start | bytes 2261000 | tf_op jit(solution)/shard_map/ppermute | solution.py:22
  230.1 13.0 %collective-permute-start.6 = (f32[23,64,128]{2,1,0:T(8,128)S(1)}, f32[23,64,128]{2,1,0:T(8,128)S(1)}, u32[]{:S(2)}, u32[]{:S(2)}) collective-permute-start(f32[23,64,128]{2,1,0:T(8,128)S(1)} %copy.66), channel_id=1, source_target_pairs={{0,4},{4,8},{8,12},{12,16},{16,20},{20,24},{24,28},{28,32},{32,36}... | collective-permute-start | bytes 2261000 | tf_op jit(solution)/shard_map/ppermute | solution.py:21
Sparse Core Ops, SparseCore 0:
  141.8 58.7 all-reduce.7
  244.9 59.1 all-reduce.9

commit v2 on v1

v2 whole, which is shorter than its diff:
```python
import functools

import jax
import jax.numpy as jnp
from jax import lax
from jax.experimental import pallas as pl
from jax.experimental.pallas import tpu as pltpu
from jax.sharding import PartitionSpec as P

ITERS = 2
HALF = 15
VIEWS = 4
SUB = 16
EDGE = 24
WIN = SUB + 2 * EDGE
CHUNKS = 4
MESH = pl.DeviceIdType.MESH
F32 = jnp.float32
BF16 = jnp.bfloat16


def split(value):
    high = value.astype(BF16)
    low = (value - high.astype(F32)).astype(BF16)
    return high, low


def dot(a, b):
    return jnp.dot(a, b, preferred_element_type=F32)


def left_pack(weights):
    high, low = split(weights)
    return jnp.concatenate([high, high, low], axis=1)


def right_pack(weights):
    high, low = split(weights)
    top = jnp.concatenate([high, low], axis=1)
    bottom = jnp.concatenate([high, jnp.zeros_like(high)], axis=1)
    return jnp.concatenate([top, bottom], axis=0)


def from_left(packed, value):
    high, low = split(value)
    return dot(packed, jnp.concatenate([high, low, high], axis=0))


def from_right(value, packed):
    high, low = split(value)
    both = dot(jnp.concatenate([high, low], axis=1), packed)
    half = both.shape[1] // 2
    return both[:, :half] + both[:, half:]


def to_lanes(rows, depth):
    return jnp.concatenate([rows[i : i + depth] for i in range(0, rows.shape[0], depth)], axis=1)


def to_rows(lanes, width):
    return jnp.concatenate([lanes[:, i : i + width] for i in range(0, lanes.shape[1], width)], axis=0)


def kernel(
    n_blk, row_size, y_cells, z_cells,
    slot_ref, mx_ref, w_ref, est_ref, view_ref,
    out_ref,
    id_own, id_row, id_all, inv_v, inv_s,
    exch, chosen, meas,
    mx_all, w_all, mxc, mxtc, wyc, wytc, wzc, wztc,
    est_half, est_flat, win, yz, stage, blurred, back_full, back_recv, corr,
    from_m1, from_p1, from_m2, from_p2, out_flat, out_half,
    id1_send, id1_recv, id2_send, id2_recv, inv_sem,
    p1_send, p1_recv, p2_send, p2_recv,
    mx_send, mx_recv, w_send, w_recv, est_send, est_recv,
    halo_send, halo_recv, x_send, x_recv, b_send, b_recv, c_send, c_recv, o_send, o_recv,
    in_row, in_plane,
):
    y_half = y_cells // 2
    y_chunk = y_half // CHUNKS
    lanes = y_chunk * z_cells
    pieces, piece_rows = view_ref.shape[0], view_ref.shape[1]
    half_pieces = pieces // 2
    n_rows = n_blk // row_size
    chips = 2 * n_blk

    x = lax.axis_index("view")
    b = lax.axis_index("blk")
    a = lax.rem(b, 2)
    c = b // 2
    other = 1 - a

    def snake(q, line):
        return q + lax.rem(line, 2) * (3 - 2 * q)

    q = snake(x, c)
    n = 4 * c + q
    partner = (x, 2 * c + other)
    row, place = b // row_size, lax.rem(b, row_size)

    def along(step):
        m = lax.rem(n + step + chips, chips)
        line = m // 4
        return (snake(lax.rem(m, 4), line), 2 * line + a)

    def device(view_blk):
        return {"view": view_blk[0], "blk": view_blk[1]}

    def remote(src, dst, send, recv, where):
        return pltpu.make_async_remote_copy(
            src_ref=src, dst_ref=dst, send_sem=send, recv_sem=recv,
            device_id=device(where), device_id_type=MESH,
        )

    def await_bytes(ref, sem):
        pltpu.make_async_copy(ref, ref, sem).wait()

    line_mates = []
    for step in range(1, 4):
        line_mates.append((lax.rem(x + step, 4), b))
    for step in range(4):
        line_mates.append((lax.rem(x + step, 4), 2 * c + other))
    chain = {step: along(step) for step in (-2, -1, 1, 2)}

    barrier = pltpu.get_barrier_semaphore()

    def greet_row(i, carry):
        mate = row * row_size + lax.rem(place + i, row_size)
        pl.semaphore_signal(barrier, inc=1, device_id=device((x, mate)), device_id_type=MESH)
        return carry

    def greet_column(i, carry):
        mate = lax.rem(row + i, n_rows) * row_size + place
        pl.semaphore_signal(barrier, inc=1, device_id=device((x, mate)), device_id_type=MESH)
        return carry

    lax.fori_loop(1, row_size, greet_row, 0)
    lax.fori_loop(1, n_rows, greet_column, 0)
    for mate in line_mates + list(chain.values()):
        pl.semaphore_signal(barrier, inc=1, device_id=device(mate), device_id_type=MESH)
    pl.semaphore_wait(barrier, row_size - 1 + n_rows - 1 + len(line_mates) + len(chain))

    def tell_column(i, carry):
        mate = lax.rem(row + i, n_rows) * row_size + place
        pl.semaphore_signal(in_row, inc=1, device_id=device((x, mate)), device_id_type=MESH)
        return carry

    lax.fori_loop(1, n_rows, tell_column, 0)

    id_own[...] = jnp.full(id_own.shape, slot_ref[0, 0], jnp.int32)

    def send_id(i, carry):
        mate = row * row_size + lax.rem(place + i, row_size)
        remote(id_own, id_row.at[place], id1_send, id1_recv, (x, mate)).start()
        return carry

    lax.fori_loop(1, row_size, send_id, 0)
    id_row[place] = id_own[...]

    par = q // 2
    rows_here = pl.ds(pl.multiple_of(lax.rem(q, 2) * SUB, SUB), SUB)

    def est_part(core):
        return est_ref.at[rows_here, pl.ds(pl.multiple_of(core * y_half, y_half), y_half), :]

    @pl.when(a == par)
    def _():
        remote(est_part(other), est_half, est_send, est_recv, partner).start()
        pltpu.make_async_copy(est_part(a), est_half, est_recv).start()

    for i, mate in enumerate(line_mates):
        remote(mx_ref, mx_all.at[a, x], mx_send.at[i], mx_recv.at[i], mate).start()
    mx_all[a, x] = mx_ref[...]
    for i in range(3):
        remote(w_ref, w_all.at[x], w_send.at[i], w_recv.at[i], line_mates[i]).start()
    w_all[x] = w_ref[...]

    pl.semaphore_wait(in_row, n_rows - 1)
    for step in range(1, 4):
        pl.semaphore_signal(
            in_plane, inc=1, device_id=device((lax.rem(x + step, 4), b)), device_id_type=MESH
        )

    def scatter(i, carry):
        to = lax.rem(b + i, n_blk)
        remote(view_ref.at[to], exch.at[b], p1_send, p1_recv, (x, to)).start()
        return carry

    lax.fori_loop(1, n_blk, scatter, 0)
    pltpu.make_async_copy(view_ref.at[b], exch.at[b], p1_recv).start()

    halo_plan = (
        (1, slice(EDGE, EDGE + SUB), slice(EDGE - SUB, EDGE)),
        (-1, slice(EDGE, EDGE + SUB), slice(EDGE + SUB, EDGE + 2 * SUB)),
        (2, slice(EDGE + SUB - 8, EDGE + SUB), slice(0, 8)),
        (-2, slice(EDGE, EDGE + 8), slice(WIN - 8, WIN)),
    )

    def halo_copies(it, ch):
        cols = slice(ch * lanes, (ch + 1) * lanes)
        return [
            remote(win.at[it, src, cols], win.at[it, dst, cols],
                   halo_send.at[it, ch, i], halo_recv.at[it, ch, i], chain[step])
            for i, (step, src, dst) in enumerate(halo_plan)
        ]

    corr_plan = (
        (1, slice(EDGE + SUB, EDGE + 2 * SUB), from_m1),
        (-1, slice(EDGE - SUB, EDGE), from_p1),
        (2, slice(WIN - 8, WIN), from_m2),
        (-2, slice(0, 8), from_p2),
    )

    def corr_copies(it, ch):
        cols = slice(ch * lanes, (ch + 1) * lanes)
        return [
            remote(corr.at[it, src, cols], dst.at[it, :, cols],
                   c_send.at[it, ch, i], c_recv.at[it, ch, i], chain[step])
            for i, (step, src, dst) in enumerate(corr_plan)
        ]

    await_bytes(est_half, est_recv)
    est_flat[...] = est_half[...].reshape(est_flat.shape)
    for ch in range(CHUNKS):
        for y in range(y_chunk):
            at = ch * y_chunk + y
            win[0, EDGE : EDGE + SUB, at * z_cells : (at + 1) * z_cells] = est_flat[
                pl.ds(at, SUB, stride=y_half), :
            ]
        for copy in halo_copies(0, ch):
            copy.start()

    await_bytes(id_row.at[: row_size - 1], id1_recv)
    padded = id_all.shape[1]
    sub = lax.broadcasted_iota(jnp.int32, (padded, 128), 0)
    ids = jnp.zeros((padded, 128), jnp.int32)
    for s in range(row_size):
        ids = jnp.where(sub == s, jnp.broadcast_to(id_row[s, 0:1, :], (padded, 128)), ids)
    id_all[row] = ids

    def send_row(i, carry):
        mate = lax.rem(row + i, n_rows) * row_size + place
        remote(id_all.at[row], id_all.at[row], id2_send, id2_recv, (x, mate)).start()
        return carry

    lax.fori_loop(1, n_rows, send_row, 0)

    for i, mate in enumerate(line_mates):
        remote(mx_ref, mx_all.at[a, x], mx_send.at[i], mx_recv.at[i], mate).wait_recv()
    mine, yours = 2 * a, 2 * other
    mat = jnp.concatenate(
        [mx_all[par, v] for v in (mine, mine + 1, yours, yours + 1)], axis=0
    )
    reach = lax.broadcasted_iota(jnp.int32, mat.shape, 1) + (n * SUB - EDGE)
    mat = jnp.where((reach >= 0) & (reach < chips * SUB), mat, F32(0.0))
    mxc[...] = left_pack(mat[:, :WIN])
    mxtc[...] = left_pack(jnp.transpose(mat)[:WIN, :])

    def blur_x(it, ch):
        for copy in halo_copies(it, ch):
            copy.wait_recv()
        out = from_left(mxc[...], win[it, :, ch * lanes : (ch + 1) * lanes])
        for y in range(y_chunk):
            part = out[:, y * z_cells : (y + 1) * z_cells]
            stage[it, ch, pl.ds(y, 2 * SUB, stride=y_chunk), :] = part[2 * SUB :]
        x_copy(it, ch).start()
        for y in range(y_chunk):
            part = out[:, y * z_cells : (y + 1) * z_cells]
            yz[it, a, ch, pl.ds(y, 2 * SUB, stride=y_chunk), :] = part[: 2 * SUB]

    def x_copy(it, ch):
        return remote(
            stage.at[it, ch], yz.at[it, a, ch], x_send.at[it, ch], x_recv.at[it, ch], partner
        )

    for ch in range(CHUNKS):
        blur_x(0, ch)

    for i in range(3):
        remote(w_ref, w_all.at[x], w_send.at[i], w_recv.at[i], line_mates[i]).wait_recv()
    for v in range(2):
        w = w_all[mine + v]
        wyc[v] = left_pack(w[:y_cells, :y_cells])
        wytc[v] = left_pack(w[:y_cells, y_cells : 2 * y_cells])
        wztc[v] = right_pack(w[y_cells : y_cells + z_cells])
        wzc[v] = right_pack(w[y_cells + z_cells :])

    await_bytes(id_all.at[: n_rows - 1], id2_recv)
    slot = lax.broadcasted_iota(jnp.int32, id_all.shape, 0) * row_size + lax.broadcasted_iota(
        jnp.int32, id_all.shape, 1
    )
    real = lax.broadcasted_iota(jnp.int32, id_all.shape, 1) < row_size
    hit = (id_all[...] == lax.broadcasted_iota(jnp.int32, id_all.shape, 2)) & real
    found = jnp.max(jnp.where(hit, slot, 0), axis=0)
    found = jnp.max(found, axis=0, keepdims=True)
    inv_v[...] = jnp.broadcast_to(found, inv_v.shape)
    to_scalars = pltpu.make_async_copy(inv_v, inv_s, inv_sem)
    to_scalars.start()
    to_scalars.wait()
    await_bytes(exch, p1_recv)
    pl.semaphore_wait(in_plane, 3)

    half = b // half_pieces
    meas_at = lax.rem(x, 2) * half_pieces + lax.rem(b, half_pieces)
    dst_piece = meas.at[pl.ds(pl.multiple_of(meas_at * piece_rows, 8), piece_rows), :]

    def forward(i, carry):
        j = lax.rem(b + i, n_blk)
        chosen[j] = exch[inv_s[0, j]]
        line = j // 2
        to_x = snake(2 * lax.rem(j, 2) + half, line)
        to_b = 2 * line + x // 2
        same = (to_x == x) & (to_b == b)

        @pl.when(same)
        def _():
            pltpu.make_async_copy(chosen.at[j], dst_piece, p2_recv).start()

        @pl.when(jnp.logical_not(same))
        def _():
            remote(chosen.at[j], dst_piece, p2_send, p2_recv, (to_x, to_b)).start()

        return carry

    lax.fori_loop(0, n_blk, forward, 0)

    group = 4

    def blur_yz(it, g):
        v = g // (SUB // group)
        rows = pl.ds(pl.multiple_of(g * (group * y_chunk), 8), group * y_chunk)
        blocks = [yz[it, h, ch, rows, :] for h in range(2) for ch in range(CHUNKS)]
        value = jnp.concatenate(
            [block[r * y_chunk : (r + 1) * y_chunk] for r in range(group) for block in blocks], axis=0
        )
        value = from_right(value, wzc[v])
        return from_left(wyc[v], to_lanes(value, y_cells))

    def back_yz(it, g, blur):
        v = g // (SUB // group)
        rows = pl.ds(pl.multiple_of(g * (group * y_cells), 8), group * y_cells)
        ratios = to_lanes(meas[rows, :], y_cells) / blur
        value = to_rows(from_left(wytc[v], ratios), z_cells)
        value = from_right(value, wztc[v])
        rows = pl.ds(pl.multiple_of(g * (group * y_half), 8), group * y_half)
        for h in range(2):
            back_full[it, h, rows, :] = jnp.concatenate(
                [value[r : r + y_half] for r in range(h * y_half, value.shape[0], y_cells)], axis=0
            )

    def back_copy(it, v):
        rows = slice(v * SUB * y_half, (v + 1) * SUB * y_half)
        return remote(
            back_full.at[it, other, rows, :], back_recv.at[it, rows, :],
            b_send.at[it, v], b_recv.at[it, v], partner,
        )

    def back_x(it, ch):
        parts = []
        for y in range(y_chunk):
            rows = pl.ds(ch * y_chunk + y, 2 * SUB, stride=y_half)
            parts.append(
                jnp.concatenate([back_full[it, a, rows, :], back_recv[it, rows, :]], axis=0)
            )
        corr[it, :, ch * lanes : (ch + 1) * lanes] = from_left(mxtc[...], jnp.concatenate(parts, axis=1))
        for copy in corr_copies(it, ch):
            copy.start()

    def updated(it, ch):
        for copy in corr_copies(it, ch):
            copy.wait_recv()
        cols = slice(ch * lanes, (ch + 1) * lanes)
        total = corr[it, EDGE : EDGE + SUB, cols] + from_m1[it, :, cols] + from_p1[it, :, cols]
        total = total + jnp.concatenate([from_m2[it, :, cols], from_p2[it, :, cols]], axis=0)
        return win[it, EDGE : EDGE + SUB, cols] * (total / VIEWS)

    def out_cols(ch, core):
        return pl.ds(pl.multiple_of(core * y_half + ch * y_chunk, 8), y_chunk)

    def out_copies(ch):
        src = out_half.at[:, ch * y_chunk : (ch + 1) * y_chunk, :]
        dst = out_ref.at[rows_here, out_cols(ch, a), :]
        own = pltpu.make_async_copy(src, dst, o_recv)
        mates = [
            remote(src, dst, o_send.at[ch, i], o_recv, (lax.rem(x + i, 4), 2 * c + par))
            for i in range(4)
        ]
        return own, mates

    for it in range(ITERS):
        for ch in range(CHUNKS):
            x_copy(it, ch).wait_recv()
        if it == 0:
            def first(g, carry):
                blurred[g] = blur_yz(0, g)
                return carry

            lax.fori_loop(0, 2 * SUB // group, first, 0)
            await_bytes(meas, p2_recv)
        per_view = SUB // group
        for v in range(2):
            def both(g, carry):
                back_yz(it, g, blurred[g] if it == 0 else blur_yz(it, g))
                return carry

            lax.fori_loop(v * per_view, (v + 1) * per_view, both, 0)
            back_copy(it, v).start()
        for v in range(2):
            back_copy(it, v).wait_recv()
        for ch in range(CHUNKS):
            back_x(it, ch)
        for ch in range(CHUNKS):
            new = updated(it, ch)
            if it + 1 < ITERS:
                win[it + 1, EDGE : EDGE + SUB, ch * lanes : (ch + 1) * lanes] = new
                for copy in halo_copies(it + 1, ch):
                    copy.start()
            else:
                for y in range(y_chunk):
                    out_flat[ch, pl.ds(y, SUB, stride=y_chunk), :] = new[
                        :, y * z_cells : (y + 1) * z_cells
                    ]
                out_half[:, ch * y_chunk : (ch + 1) * y_chunk, :] = out_flat[ch].reshape(
                    SUB, y_chunk, z_cells
                )
                own, mates = out_copies(ch)
                for mate in mates[1:]:
                    mate.start()

                @pl.when(a == par)
                def _():
                    own.start()

                @pl.when(a != par)
                def _():
                    mates[0].start()
        if it + 1 < ITERS:
            for ch in range(CHUNKS):
                blur_x(it + 1, ch)

    await_bytes(id_row.at[: row_size - 1], id1_send)
    await_bytes(id_all.at[: n_rows - 1], id2_send)
    await_bytes(exch.at[: n_blk - 1], p1_send)
    await_bytes(chosen.at[: n_blk - 1], p2_send)

    @pl.when(jnp.logical_not((a == x // 2) & (lax.rem(q, 2) == half)))
    def _():
        await_bytes(chosen.at[0], p2_send)

    @pl.when(a == par)
    def _():
        remote(est_part(other), est_half, est_send, est_recv, partner).wait_send()

    for i, mate in enumerate(line_mates):
        remote(mx_ref, mx_all.at[a, x], mx_send.at[i], mx_recv.at[i], mate).wait_send()
    for i in range(3):
        remote(w_ref, w_all.at[x], w_send.at[i], w_recv.at[i], line_mates[i]).wait_send()
    for it in range(ITERS):
        for ch in range(CHUNKS):
            for copy in halo_copies(it, ch) + corr_copies(it, ch) + [x_copy(it, ch)]:
                copy.wait_send()
        for v in range(2):
            back_copy(it, v).wait_send()
    for ch in range(CHUNKS):
        own, mates = out_copies(ch)
        for mate in mates[1:]:
            mate.wait_send()

        @pl.when(a != par)
        def _():
            mates[0].wait_send()

    await_bytes(out_ref, o_recv)


def banded(weights, offsets_table):
    hits = offsets_table[..., None] == jnp.arange(weights.shape[0], dtype=jnp.int32)
    return jnp.sum(jnp.where(hits, weights, F32(0.0)), axis=-1)


def shifts(rows, columns):
    return jnp.arange(columns, dtype=jnp.int32)[None, :] - jnp.arange(rows, dtype=jnp.int32)[:, None]


def per_device(estimate, view_data, slot_block, offsets, taps):
    n_blk = lax.axis_size("blk")
    block_rows, y_cells, z_cells = estimate.shape
    row_size = 16 if n_blk % 16 == 0 else n_blk // 2
    n_rows = n_blk // row_size
    padded = max(row_size, 8)
    piece_rows = block_rows * y_cells // n_blk
    weights = taps[0] / jnp.sum(taps[0], axis=-1, keepdims=True)
    mat_x = banded(weights[0], shifts(SUB, 128) - (EDGE - HALF) - offsets[0, 0])
    mat_y = banded(weights[1], shifts(y_cells, y_cells) + HALF)
    mat_z = banded(weights[2], shifts(z_cells, z_cells) + HALF)
    tables = jnp.concatenate(
        [jnp.concatenate([mat_y, mat_y.T], axis=1), mat_z, mat_z.T], axis=0
    )
    pieces = view_data.reshape(n_blk, piece_rows, z_cells)
    y_half = y_cells // 2
    y_chunk = y_half // CHUNKS
    width = y_half * z_cells
    vmem = pltpu.VMEM
    dma = pltpu.SemaphoreType.DMA
    regular = pltpu.SemaphoreType.REGULAR
    return pl.pallas_call(
        functools.partial(kernel, n_blk, row_size, y_cells, z_cells),
        out_shape=jax.ShapeDtypeStruct(estimate.shape, F32),
        in_specs=[
            pl.BlockSpec(memory_space=pltpu.SMEM),
            pl.BlockSpec(memory_space=pltpu.VMEM),
            pl.BlockSpec(memory_space=pltpu.VMEM),
            pl.BlockSpec(memory_space=pl.ANY),
            pl.BlockSpec(memory_space=pl.ANY),
        ],
        out_specs=pl.BlockSpec(memory_space=pl.ANY),
        scratch_shapes=[
            vmem((8, 128), jnp.int32),
            vmem((row_size, 8, 128), jnp.int32),
            vmem((n_rows, padded, 128), jnp.int32),
            vmem((8, 128), jnp.int32),
            pltpu.SMEM((8, 128), jnp.int32),
            vmem((n_blk, piece_rows, z_cells), F32),
            vmem((n_blk, piece_rows, z_cells), F32),
            vmem((2 * SUB * y_cells, z_cells), F32),
            vmem((2, VIEWS, SUB, 128), F32),
            vmem((VIEWS,) + tables.shape, F32),
            vmem((4 * SUB, 3 * WIN), BF16),
            vmem((WIN, 3 * 4 * SUB), BF16),
            vmem((2, y_cells, 3 * y_cells), BF16),
            vmem((2, y_cells, 3 * y_cells), BF16),
            vmem((2, 2 * z_cells, 2 * z_cells), BF16),
            vmem((2, 2 * z_cells, 2 * z_cells), BF16),
            vmem((SUB, y_half, z_cells), F32),
            vmem((SUB * y_half, z_cells), F32),
            vmem((ITERS, WIN, width), F32),
            vmem((ITERS, 2, CHUNKS, 2 * SUB * y_chunk, z_cells), F32),
            vmem((ITERS, CHUNKS, 2 * SUB * y_chunk, z_cells), F32),
            vmem((2 * SUB // 4, y_cells, 4 * z_cells), F32),
            vmem((ITERS, 2, 2 * SUB * y_half, z_cells), F32),
            vmem((ITERS, 2 * SUB * y_half, z_cells), F32),
            vmem((ITERS, WIN, width), F32),
            vmem((ITERS, SUB, width), F32),
            vmem((ITERS, SUB, width), F32),
            vmem((ITERS, 8, width), F32),
            vmem((ITERS, 8, width), F32),
            vmem((CHUNKS, SUB * y_chunk, z_cells), F32),
            vmem((SUB, y_half, z_cells), F32),
            dma, dma, dma, dma, dma,
            dma, dma, dma, dma,
            dma((7,)), dma((7,)), dma((3,)), dma((3,)), dma, dma,
            dma((ITERS, CHUNKS, 4)), dma((ITERS, CHUNKS, 4)),
            dma((ITERS, CHUNKS)), dma((ITERS, CHUNKS)),
            dma((ITERS, 2)), dma((ITERS, 2)),
            dma((ITERS, CHUNKS, 4)), dma((ITERS, CHUNKS, 4)),
            dma((CHUNKS, 4)), dma,
            regular, regular,
        ],
        compiler_params=pltpu.CompilerParams(
            collective_id=0, has_side_effects=True, vmem_limit_bytes=48 * 1024 * 1024
        ),
    )(slot_block, mat_x, tables, estimate, pieces)


def solution(mesh):
    return jax.shard_map(
        per_device,
        mesh=mesh,
        in_specs=(
            P("blk", None, None),
            P("view", "blk", None, None),
            P("view", "blk"),
            P("view", "blk"),
            P("view", None, None),
        ),
        out_specs=P("blk", None, None),
        check_vma=False,
    )
```

time: 315 us -> 170 us (0.54)
  waiting for transfers between devices: 164 us -> 0 us
  Pallas kernels: 0 us -> 163 us
  starting transfers between devices: 56.6 us -> 0 us
  blocking collectives: 37.9 us -> 0 us
  matrix products: 17.8 us -> 0 us
  between operations: 15.1 us -> 1.36 us
  local copies, waits for them, and re-layouts: 15.9 us -> 3.59 us
  other arithmetic: 6.72 us -> 2.22 us
    pallas_call x0 -> x1, Pallas kernels: none -> 163 us  [per_device(): pl.pallas_call(functools.partial(kernel, n_blk, row_size, y_cells, z_cell...]
    psum x2 -> x0, waiting for transfers between devices: 118 us -> none  [per_device(): summed = lax.psum(own_rows, 'view')]
    ppermute x8 -> x0, waiting for transfers between devices: 45.7 us -> none  [the longest x4 24 us: extended_2(): before = lax.ppermute(last, axis, up)]
    unnamed x1 -> x0, blocking collectives: 37.9 us -> none
    all_to_all x2 -> x0, starting transfers between devices: 31.3 us -> none  [the longest x1 18.4 us: relay_blocks(): lax.all_to_all(pieces, 'blk', split_axis=0, concat_axis=0, tiled=True)]
    ppermute x8 -> x0, starting transfers between devices: 25.2 us -> none  [the longest x4 15.3 us: extended_2(): before = lax.ppermute(last, axis, up)]
    dot_general x12 -> x0, matrix products: 17.8 us -> none  [the longest x2 5.43 us: per_device(): back_w = jnp.einsum('xw,xyz->wyz', mat_x, back_y, precision=HIGHEST)]
    ppermute x8 -> x0, local copies, waits for them, and re-layouts: 5.78 us -> none  [the longest x4 2.89 us: extended_2(): after = lax.ppermute(leading, axis, down)]
  transfers between devices with their start and end apart: 12 -> 0, of which waited for: 10 -> 0; matrix products, arithmetic and copies ran while one was open for 4% -> 0% of each run, Pallas kernels for 0% -> 0%
where the time goes in v2:
time: 170 us
  Pallas kernels  163 us (96%)
  local copies, waits for them, and re-layouts  3.59 us (2%)
  other arithmetic  2.22 us (1%)
    pallas_call x1, Pallas kernels, per_device(): pl.pallas_call(functools.partial(kernel, n_blk, row_size, y_cells, z_cell...  163 us
    unnamed x5, local copies, waits for them, and re-layouts  3.43 us

profile of v2, /device:TPU:1, one launch (start us, length us, event | category | flops | bytes accessed | tf_op | source)
XLA Modules:
  0.0 169.9 jit_solution(4712702287837407014)
XLA Ops:
  1.3 0.8 reduce_sum.36
  2.1 0.8 bitcast_divide_fusion
  2.9 0.1 select_reduce_fusion.2.mx_ref
  3.0 0.2 select_reduce_fusion.1
  3.2 0.1 copy.8
  3.3 0.3 select_reduce_fusion
  3.6 0.1 copy.9
  3.6 0.1 pad_maximum_fusion.w_ref
  3.7 0.0 copy-start
  3.7 1.2 copy-done
  5.0 0.0 copy-start.1
  5.0 1.2 copy-done.1
  6.2 162.8 %shard_map.55 = f32[32,64,128]{2,1,0:T(8,128)S(1)} custom-call(s32[1,1]{1,0:T(1,128)S(6)} %copy.13.slot_ref, f32[16,128]{1,0:T(8,128)S(1)} %select_reduce_fusion.2.mx_ref, f32[320,128]{1,0:T(8,128)S(1)} %pad_maximum_fusion.w_ref, f32[32,64,128]{2,1,0:T(8,128)S(1)} %copy-done, f32[128,16,128]{2,1,0:T(8,128)S(1)} %bitcast.13), custom_call_target="tpu_custom_call" | custom-call | tf_op jit(solution)/shard_map/pallas_call | solution.py:506
  169.0 1.0 copy.15
  (4 shorter events, 0.0 us)
Async XLA Ops:
  3.7 1.2 copy-start
  5.0 1.2 copy-start.1

commit v3 on v2

--- a/solution.py
+++ b/solution.py
@@ -14,6 +14,7 @@
 EDGE = 24
 WIN = SUB + 2 * EDGE
 CHUNKS = 4
+STRIDE = 45
 MESH = pl.DeviceIdType.MESH
 F32 = jnp.float32
 BF16 = jnp.bfloat16
@@ -63,16 +64,16 @@
 
 def kernel(
     n_blk, row_size, y_cells, z_cells,
-    slot_ref, mx_ref, w_ref, est_ref, view_ref,
+    slot_ref, off_ref, taps_ref, est_ref, view_ref,
     out_ref,
     id_own, id_row, id_all, inv_v, inv_s,
     exch, chosen, meas,
-    mx_all, w_all, mxc, mxtc, wyc, wytc, wzc, wztc,
+    prm, prm_all, mxc, mxtc, wyc, wytc, wzc, wztc,
     est_half, est_flat, win, yz, stage, blurred, back_full, back_recv, corr,
     from_m1, from_p1, from_m2, from_p2, out_flat, out_half,
     id1_send, id1_recv, id2_send, id2_recv, inv_sem,
     p1_send, p1_recv, p2_send, p2_recv,
-    mx_send, mx_recv, w_send, w_recv, est_send, est_recv,
+    prm_send, prm_recv, est_send, est_recv,
     halo_send, halo_recv, x_send, x_recv, b_send, b_recv, c_send, c_recv, o_send, o_recv,
     in_row, in_plane,
 ):
@@ -115,6 +116,10 @@
     def await_bytes(ref, sem):
         pltpu.make_async_copy(ref, ref, sem).wait()
 
+    taps = taps_ref[0]
+    prm[...] = jnp.zeros(prm.shape, F32) + off_ref[0, 0].astype(F32)
+    prm[0:3, 0 : taps.shape[1]] = taps / jnp.sum(taps, axis=1, keepdims=True)
+
     line_mates = []
     for step in range(1, 4):
         line_mates.append((lax.rem(x + step, 4), b))
@@ -122,6 +127,11 @@
         line_mates.append((lax.rem(x + step, 4), 2 * c + other))
     chain = {step: along(step) for step in (-2, -1, 1, 2)}
 
+    prm_copies = [
+        remote(prm, prm_all.at[a, x], prm_send.at[i], prm_recv.at[i], mate)
+        for i, mate in enumerate(line_mates)
+    ]
+
     barrier = pltpu.get_barrier_semaphore()
 
     def greet_row(i, carry):
@@ -168,12 +178,9 @@
         remote(est_part(other), est_half, est_send, est_recv, partner).start()
         pltpu.make_async_copy(est_part(a), est_half, est_recv).start()
 
-    for i, mate in enumerate(line_mates):
-        remote(mx_ref, mx_all.at[a, x], mx_send.at[i], mx_recv.at[i], mate).start()
-    mx_all[a, x] = mx_ref[...]
-    for i in range(3):
-        remote(w_ref, w_all.at[x], w_send.at[i], w_recv.at[i], line_mates[i]).start()
-    w_all[x] = w_ref[...]
+    for copy in prm_copies:
+        copy.start()
+    prm_all[a, x] = prm[...]
 
     pl.semaphore_wait(in_row, n_rows - 1)
     for step in range(1, 4):
@@ -182,7 +189,7 @@
         )
 
     def scatter(i, carry):
-        to = lax.rem(b + i, n_blk)
+        to = lax.rem(b + i * STRIDE, n_blk)
         remote(view_ref.at[to], exch.at[b], p1_send, p1_recv, (x, to)).start()
         return carry
 
@@ -244,17 +251,6 @@
         return carry
 
     lax.fori_loop(1, n_rows, send_row, 0)
-
-    for i, mate in enumerate(line_mates):
-        remote(mx_ref, mx_all.at[a, x], mx_send.at[i], mx_recv.at[i], mate).wait_recv()
-    mine, yours = 2 * a, 2 * other
-    mat = jnp.concatenate(
-        [mx_all[par, v] for v in (mine, mine + 1, yours, yours + 1)], axis=0
-    )
-    reach = lax.broadcasted_iota(jnp.int32, mat.shape, 1) + (n * SUB - EDGE)
-    mat = jnp.where((reach >= 0) & (reach < chips * SUB), mat, F32(0.0))
-    mxc[...] = left_pack(mat[:, :WIN])
-    mxtc[...] = left_pack(jnp.transpose(mat)[:WIN, :])
 
     def blur_x(it, ch):
         for copy in halo_copies(it, ch):
@@ -272,18 +268,6 @@
         return remote(
             stage.at[it, ch], yz.at[it, a, ch], x_send.at[it, ch], x_recv.at[it, ch], partner
         )
-
-    for ch in range(CHUNKS):
-        blur_x(0, ch)
-
-    for i in range(3):
-        remote(w_ref, w_all.at[x], w_send.at[i], w_recv.at[i], line_mates[i]).wait_recv()
-    for v in range(2):
-        w = w_all[mine + v]
-        wyc[v] = left_pack(w[:y_cells, :y_cells])
-        wytc[v] = left_pack(w[:y_cells, y_cells : 2 * y_cells])
-        wztc[v] = right_pack(w[y_cells : y_cells + z_cells])
-        wzc[v] = right_pack(w[y_cells + z_cells :])
 
     await_bytes(id_all.at[: n_rows - 1], id2_recv)
     slot = lax.broadcasted_iota(jnp.int32, id_all.shape, 0) * row_size + lax.broadcasted_iota(
@@ -305,7 +289,7 @@
     dst_piece = meas.at[pl.ds(pl.multiple_of(meas_at * piece_rows, 8), piece_rows), :]
 
     def forward(i, carry):
-        j = lax.rem(b + i, n_blk)
+        j = lax.rem(b + i * STRIDE, n_blk)
         chosen[j] = exch[inv_s[0, j]]
         line = j // 2
         to_x = snake(2 * lax.rem(j, 2) + half, line)
@@ -323,6 +307,42 @@
         return carry
 
     lax.fori_loop(0, n_blk, forward, 0)
+
+    for copy in prm_copies:
+        copy.wait_recv()
+    n_taps = taps.shape[1]
+    mine, yours = 2 * a, 2 * other
+
+    def band(shift, weights):
+        value = jnp.zeros(shift.shape, F32)
+        for u in range(n_taps):
+            value = jnp.where(shift == u, weights[:, u : u + 1], value)
+        return value
+
+    def iota(shape, dim):
+        return lax.broadcasted_iota(jnp.int32, shape, dim)
+
+    tiles = [prm_all[par, v] for v in (mine, mine + 1, yours, yours + 1)]
+    shape = (SUB, 128)
+    base = iota(shape, 1) - iota(shape, 0) - (EDGE - HALF)
+    mat = jnp.concatenate(
+        [band(base.astype(F32) - tile[3:4, :], tile[0:1, :]) for tile in tiles], axis=0
+    )
+    reach = iota(mat.shape, 1) + (n * SUB - EDGE)
+    mat = jnp.where((reach >= 0) & (reach < chips * SUB), mat, F32(0.0))
+    mxc[...] = left_pack(mat[:, :WIN])
+    mxtc[...] = left_pack(jnp.transpose(mat)[:WIN, :])
+    for v in range(2):
+        for cells, row, forth, back, pack in (
+            (y_cells, 1, wyc, wytc, left_pack), (z_cells, 2, wztc, wzc, right_pack),
+        ):
+            shape = (cells, cells)
+            apart = iota(shape, 1) - iota(shape, 0)
+            forth[v] = pack(band(apart + HALF, tiles[v][row : row + 1, :]))
+            back[v] = pack(band(HALF - apart, tiles[v][row : row + 1, :]))
+
+    for ch in range(CHUNKS):
+        blur_x(0, ch)
 
     group = 4
 
@@ -451,10 +471,8 @@
     def _():
         remote(est_part(other), est_half, est_send, est_recv, partner).wait_send()
 
-    for i, mate in enumerate(line_mates):
-        remote(mx_ref, mx_all.at[a, x], mx_send.at[i], mx_recv.at[i], mate).wait_send()
-    for i in range(3):
-        remote(w_ref, w_all.at[x], w_send.at[i], w_recv.at[i], line_mates[i]).wait_send()
+    for copy in prm_copies:
+        copy.wait_send()
     for it in range(ITERS):
         for ch in range(CHUNKS):
             for copy in halo_copies(it, ch) + corr_copies(it, ch) + [x_copy(it, ch)]:
@@ -473,15 +491,6 @@
     await_bytes(out_ref, o_recv)
 
 
-def banded(weights, offsets_table):
-    hits = offsets_table[..., None] == jnp.arange(weights.shape[0], dtype=jnp.int32)
-    return jnp.sum(jnp.where(hits, weights, F32(0.0)), axis=-1)
-
-
-def shifts(rows, columns):
-    return jnp.arange(columns, dtype=jnp.int32)[None, :] - jnp.arange(rows, dtype=jnp.int32)[:, None]
-
-
 def per_device(estimate, view_data, slot_block, offsets, taps):
     n_blk = lax.axis_size("blk")
     block_rows, y_cells, z_cells = estimate.shape
@@ -489,13 +498,6 @@
     n_rows = n_blk // row_size
     padded = max(row_size, 8)
     piece_rows = block_rows * y_cells // n_blk
-    weights = taps[0] / jnp.sum(taps[0], axis=-1, keepdims=True)
-    mat_x = banded(weights[0], shifts(SUB, 128) - (EDGE - HALF) - offsets[0, 0])
-    mat_y = banded(weights[1], shifts(y_cells, y_cells) + HALF)
-    mat_z = banded(weights[2], shifts(z_cells, z_cells) + HALF)
-    tables = jnp.concatenate(
-        [jnp.concatenate([mat_y, mat_y.T], axis=1), mat_z, mat_z.T], axis=0
-    )
     pieces = view_data.reshape(n_blk, piece_rows, z_cells)
     y_half = y_cells // 2
     y_chunk = y_half // CHUNKS
@@ -508,7 +510,7 @@
         out_shape=jax.ShapeDtypeStruct(estimate.shape, F32),
         in_specs=[
             pl.BlockSpec(memory_space=pltpu.SMEM),
-            pl.BlockSpec(memory_space=pltpu.VMEM),
+            pl.BlockSpec(memory_space=pltpu.SMEM),
             pl.BlockSpec(memory_space=pltpu.VMEM),
             pl.BlockSpec(memory_space=pl.ANY),
             pl.BlockSpec(memory_space=pl.ANY),
@@ -523,8 +525,8 @@
             vmem((n_blk, piece_rows, z_cells), F32),
             vmem((n_blk, piece_rows, z_cells), F32),
             vmem((2 * SUB * y_cells, z_cells), F32),
-            vmem((2, VIEWS, SUB, 128), F32),
-            vmem((VIEWS,) + tables.shape, F32),
+            vmem((8, 128), F32),
+            vmem((2, VIEWS, 8, 128), F32),
             vmem((4 * SUB, 3 * WIN), BF16),
             vmem((WIN, 3 * 4 * SUB), BF16),
             vmem((2, y_cells, 3 * y_cells), BF16),
@@ -548,7 +550,7 @@
             vmem((SUB, y_half, z_cells), F32),
             dma, dma, dma, dma, dma,
             dma, dma, dma, dma,
-            dma((7,)), dma((7,)), dma((3,)), dma((3,)), dma, dma,
+            dma((7,)), dma((7,)), dma, dma,
             dma((ITERS, CHUNKS, 4)), dma((ITERS, CHUNKS, 4)),
             dma((ITERS, CHUNKS)), dma((ITERS, CHUNKS)),
             dma((ITERS, 2)), dma((ITERS, 2)),
@@ -557,9 +559,9 @@
             regular, regular,
         ],
         compiler_params=pltpu.CompilerParams(
-            collective_id=0, has_side_effects=True, vmem_limit_bytes=48 * 1024 * 1024
+            collective_id=0, has_side_effects=True, vmem_limit_bytes=52 * 1024 * 1024
         ),
-    )(slot_block, mat_x, tables, estimate, pieces)
+    )(slot_block, offsets, taps, estimate, pieces)
 
 
 def solution(mesh):

time: 170 us -> 145 us (0.85); the launches traced: 170 us -> 143 us
  Pallas kernels: 163 us -> 141 us
  local copies, waits for them, and re-layouts: 3.59 us -> 0.99 us
  other arithmetic: 2.22 us -> 0 us
    pallas_call x1, Pallas kernels: 163 us -> 141 us  [per_device(): pl.pallas_call(functools.partial(kernel, n_blk, row_size, y_cells, z_cell...]
    unnamed x5 -> x4, local copies, waits for them, and re-layouts: 3.43 us -> 0.99 us
where the time goes in v3:
time: 145 us; the launch traced here: 143 us
  Pallas kernels  141 us (97%)
    pallas_call x1, Pallas kernels, per_device(): pl.pallas_call(functools.partial(kernel, n_blk, row_size, y_cells, z_cell...  141 us

profile of v3, /device:TPU:1, one launch (start us, length us, event | category | flops | bytes accessed | tf_op | source)
XLA Modules:
  0.0 143.2 jit_solution(1096551915783410159)
XLA Ops:
  0.7 0.0 copy-start
  1.3 0.0 copy-done
  1.3 140.8 %shard_map.55 = f32[32,64,128]{2,1,0:T(8,128)S(1)} custom-call(s32[1,1]{1,0:T(1,128)S(6)} %copy.8.slot_ref, s32[1,1]{1,0:T(1,128)S(6)} %copy.9.off_ref, f32[1,3,31]{2,1,0:T(4,128)S(1)} %copy.6.taps_ref, f32[32,64,128]{2,1,0:T(8,128)} %est_ref.1, f32[128,16,128]{2,1,0:T(8,128)} %bitcast.1), custom_call_target="tpu_custom_call" | custom-call | tf_op jit(solution)/shard_map/pallas_call | solution.py:508
  142.2 1.0 copy.10
  (1 shorter events, 0.0 us)
Async XLA Ops:
  0.7 0.7 copy-start

commit v4 on v3

--- a/solution.py
+++ b/solution.py
@@ -13,7 +13,8 @@
 SUB = 16
 EDGE = 24
 WIN = SUB + 2 * EDGE
-CHUNKS = 4
+CHUNKS = 2
+EARLY = 33
 STRIDE = 45
 MESH = pl.DeviceIdType.MESH
 F32 = jnp.float32
@@ -70,11 +71,11 @@
     exch, chosen, meas,
     prm, prm_all, mxc, mxtc, wyc, wytc, wzc, wztc,
     est_half, est_flat, win, yz, stage, blurred, back_full, back_recv, corr,
-    from_m1, from_p1, from_m2, from_p2, out_flat, out_half,
+    came, merged, out_flat, out_half,
     id1_send, id1_recv, id2_send, id2_recv, inv_sem,
     p1_send, p1_recv, p2_send, p2_recv,
     prm_send, prm_recv, est_send, est_recv,
-    halo_send, halo_recv, x_send, x_recv, b_send, b_recv, c_send, c_recv, o_send, o_recv,
+    halo_send, halo_recv, x_send, x_recv, b_send, b_recv, c_send, c_recv, o_send, f_send, o_recv,
     in_row, in_plane,
 ):
     y_half = y_cells // 2
@@ -104,6 +105,23 @@
         line = m // 4
         return (snake(lax.rem(m, 4), line), 2 * line + a)
 
+    last = chips - 1
+
+    def send_along(step, copy):
+        @pl.when(n != (last if step > 0 else 0))
+        def _():
+            copy.start()
+
+    def sent_along(step, copy):
+        @pl.when(n != (last if step > 0 else 0))
+        def _():
+            copy.wait_send()
+
+    def take_along(step, copy):
+        @pl.when(n != (0 if step > 0 else last))
+        def _():
+            copy.wait_recv()
+
     def device(view_blk):
         return {"view": view_blk[0], "blk": view_blk[1]}
 
@@ -116,6 +134,11 @@
     def await_bytes(ref, sem):
         pltpu.make_async_copy(ref, ref, sem).wait()
 
+    @pl.when((n == 0) | (n == last))
+    def _():
+        win[...] = jnp.zeros(win.shape, F32)
+        came[...] = jnp.zeros(came.shape, F32)
+
     taps = taps_ref[0]
     prm[...] = jnp.zeros(prm.shape, F32) + off_ref[0, 0].astype(F32)
     prm[0:3, 0 : taps.shape[1]] = taps / jnp.sum(taps, axis=1, keepdims=True)
@@ -125,7 +148,7 @@
         line_mates.append((lax.rem(x + step, 4), b))
     for step in range(4):
         line_mates.append((lax.rem(x + step, 4), 2 * c + other))
-    chain = {step: along(step) for step in (-2, -1, 1, 2)}
+    chain = {step: along(step) for step in (-1, 1)}
 
     prm_copies = [
         remote(prm, prm_all.at[a, x], prm_send.at[i], prm_recv.at[i], mate)
@@ -146,9 +169,9 @@
 
     lax.fori_loop(1, row_size, greet_row, 0)
     lax.fori_loop(1, n_rows, greet_column, 0)
-    for mate in line_mates + list(chain.values()):
+    for mate in line_mates:
         pl.semaphore_signal(barrier, inc=1, device_id=device(mate), device_id_type=MESH)
-    pl.semaphore_wait(barrier, row_size - 1 + n_rows - 1 + len(line_mates) + len(chain))
+    pl.semaphore_wait(barrier, row_size - 1 + n_rows - 1 + len(line_mates))
 
     def tell_column(i, carry):
         mate = lax.rem(row + i, n_rows) * row_size + place
@@ -193,38 +216,54 @@
         remote(view_ref.at[to], exch.at[b], p1_send, p1_recv, (x, to)).start()
         return carry
 
-    lax.fori_loop(1, n_blk, scatter, 0)
-    pltpu.make_async_copy(view_ref.at[b], exch.at[b], p1_recv).start()
+    early = min(EARLY, n_blk)
+    lax.fori_loop(1, early, scatter, 0)
 
     halo_plan = (
-        (1, slice(EDGE, EDGE + SUB), slice(EDGE - SUB, EDGE)),
-        (-1, slice(EDGE, EDGE + SUB), slice(EDGE + SUB, EDGE + 2 * SUB)),
-        (2, slice(EDGE + SUB - 8, EDGE + SUB), slice(0, 8)),
-        (-2, slice(EDGE, EDGE + 8), slice(WIN - 8, WIN)),
+        (1, EDGE + 8, EDGE - 8), (-1, EDGE, EDGE + SUB),
+        (1, EDGE, EDGE - SUB), (-1, EDGE + 8, EDGE + SUB + 8),
+        (1, EDGE - 8, 0), (-1, EDGE + SUB, WIN - 8),
     )
 
     def halo_copies(it, ch):
         cols = slice(ch * lanes, (ch + 1) * lanes)
         return [
-            remote(win.at[it, src, cols], win.at[it, dst, cols],
+            remote(win.at[it, src : src + 8, cols], win.at[it, dst : dst + 8, cols],
                    halo_send.at[it, ch, i], halo_recv.at[it, ch, i], chain[step])
             for i, (step, src, dst) in enumerate(halo_plan)
         ]
 
+    def pass_on(it, ch):
+        copies = halo_copies(it, ch)
+        for i in range(2):
+            step = halo_plan[i][0]
+            take_along(step, copies[i])
+            send_along(step, copies[4 + i])
+
     corr_plan = (
-        (1, slice(EDGE + SUB, EDGE + 2 * SUB), from_m1),
-        (-1, slice(EDGE - SUB, EDGE), from_p1),
-        (2, slice(WIN - 8, WIN), from_m2),
-        (-2, slice(0, 8), from_p2),
+        (1, WIN - 8), (-1, 0),
+        (1, EDGE + SUB + 8), (-1, EDGE - SUB),
+        (1, EDGE + SUB), (-1, EDGE - 8),
     )
 
     def corr_copies(it, ch):
         cols = slice(ch * lanes, (ch + 1) * lanes)
-        return [
-            remote(corr.at[it, src, cols], dst.at[it, :, cols],
-                   c_send.at[it, ch, i], c_recv.at[it, ch, i], chain[step])
-            for i, (step, src, dst) in enumerate(corr_plan)
-        ]
+        copies = []
+        for i, (step, src) in enumerate(corr_plan):
+            here = corr.at[it, src : src + 8, cols] if i < 4 else merged.at[it, i - 4, :, cols]
+            copies.append(
+                remote(here, came.at[it, i, :, cols], c_send.at[it, ch, i], c_recv.at[it, ch, i], chain[step])
+            )
+        return copies
+
+    def merge(it, ch):
+        cols = slice(ch * lanes, (ch + 1) * lanes)
+        copies = corr_copies(it, ch)
+        for i in range(2):
+            step, src = corr_plan[4 + i]
+            take_along(step, copies[i])
+            merged[it, i, :, cols] = corr[it, src : src + 8, cols] + came[it, i, :, cols]
+            send_along(step, copies[4 + i])
 
     await_bytes(est_half, est_recv)
     est_flat[...] = est_half[...].reshape(est_flat.shape)
@@ -234,8 +273,11 @@
             win[0, EDGE : EDGE + SUB, at * z_cells : (at + 1) * z_cells] = est_flat[
                 pl.ds(at, SUB, stride=y_half), :
             ]
-        for copy in halo_copies(0, ch):
-            copy.start()
+        for i, copy in enumerate(halo_copies(0, ch)[:4]):
+            send_along(halo_plan[i][0], copy)
+
+    lax.fori_loop(early, n_blk, scatter, 0)
+    pltpu.make_async_copy(view_ref.at[b], exch.at[b], p1_recv).start()
 
     await_bytes(id_row.at[: row_size - 1], id1_recv)
     padded = id_all.shape[1]
@@ -253,8 +295,8 @@
     lax.fori_loop(1, n_rows, send_row, 0)
 
     def blur_x(it, ch):
-        for copy in halo_copies(it, ch):
-            copy.wait_recv()
+        for i, copy in enumerate(halo_copies(it, ch)[2:]):
+            take_along(halo_plan[2 + i][0], copy)
         out = from_left(mxc[...], win[it, :, ch * lanes : (ch + 1) * lanes])
         for y in range(y_chunk):
             part = out[:, y * z_cells : (y + 1) * z_cells]
@@ -268,45 +310,6 @@
         return remote(
             stage.at[it, ch], yz.at[it, a, ch], x_send.at[it, ch], x_recv.at[it, ch], partner
         )
-
-    await_bytes(id_all.at[: n_rows - 1], id2_recv)
-    slot = lax.broadcasted_iota(jnp.int32, id_all.shape, 0) * row_size + lax.broadcasted_iota(
-        jnp.int32, id_all.shape, 1
-    )
-    real = lax.broadcasted_iota(jnp.int32, id_all.shape, 1) < row_size
-    hit = (id_all[...] == lax.broadcasted_iota(jnp.int32, id_all.shape, 2)) & real
-    found = jnp.max(jnp.where(hit, slot, 0), axis=0)
-    found = jnp.max(found, axis=0, keepdims=True)
-    inv_v[...] = jnp.broadcast_to(found, inv_v.shape)
-    to_scalars = pltpu.make_async_copy(inv_v, inv_s, inv_sem)
-    to_scalars.start()
-    to_scalars.wait()
-    await_bytes(exch, p1_recv)
-    pl.semaphore_wait(in_plane, 3)
-
-    half = b // half_pieces
-    meas_at = lax.rem(x, 2) * half_pieces + lax.rem(b, half_pieces)
-    dst_piece = meas.at[pl.ds(pl.multiple_of(meas_at * piece_rows, 8), piece_rows), :]
-
-    def forward(i, carry):
-        j = lax.rem(b + i * STRIDE, n_blk)
-        chosen[j] = exch[inv_s[0, j]]
-        line = j // 2
-        to_x = snake(2 * lax.rem(j, 2) + half, line)
-        to_b = 2 * line + x // 2
-        same = (to_x == x) & (to_b == b)
-
-        @pl.when(same)
-        def _():
-            pltpu.make_async_copy(chosen.at[j], dst_piece, p2_recv).start()
-
-        @pl.when(jnp.logical_not(same))
-        def _():
-            remote(chosen.at[j], dst_piece, p2_send, p2_recv, (to_x, to_b)).start()
-
-        return carry
-
-    lax.fori_loop(0, n_blk, forward, 0)
 
     for copy in prm_copies:
         copy.wait_recv()
@@ -342,7 +345,48 @@
             back[v] = pack(band(HALF - apart, tiles[v][row : row + 1, :]))
 
     for ch in range(CHUNKS):
+        pass_on(0, ch)
+    for ch in range(CHUNKS):
         blur_x(0, ch)
+
+    await_bytes(id_all.at[: n_rows - 1], id2_recv)
+    slot = lax.broadcasted_iota(jnp.int32, id_all.shape, 0) * row_size + lax.broadcasted_iota(
+        jnp.int32, id_all.shape, 1
+    )
+    real = lax.broadcasted_iota(jnp.int32, id_all.shape, 1) < row_size
+    hit = (id_all[...] == lax.broadcasted_iota(jnp.int32, id_all.shape, 2)) & real
+    found = jnp.max(jnp.where(hit, slot, 0), axis=0)
+    found = jnp.max(found, axis=0, keepdims=True)
+    inv_v[...] = jnp.broadcast_to(found, inv_v.shape)
+    to_scalars = pltpu.make_async_copy(inv_v, inv_s, inv_sem)
+    to_scalars.start()
+    to_scalars.wait()
+    await_bytes(exch, p1_recv)
+    pl.semaphore_wait(in_plane, 3)
+
+    half = b // half_pieces
+    meas_at = lax.rem(x, 2) * half_pieces + lax.rem(b, half_pieces)
+    dst_piece = meas.at[pl.ds(pl.multiple_of(meas_at * piece_rows, 8), piece_rows), :]
+
+    def forward(i, carry):
+        j = lax.rem(b + i * STRIDE, n_blk)
+        chosen[j] = exch[inv_s[0, j]]
+        line = j // 2
+        to_x = snake(2 * lax.rem(j, 2) + half, line)
+        to_b = 2 * line + x // 2
+        same = (to_x == x) & (to_b == b)
+
+        @pl.when(same)
+        def _():
+            pltpu.make_async_copy(chosen.at[j], dst_piece, p2_recv).start()
+
+        @pl.when(jnp.logical_not(same))
+        def _():
+            remote(chosen.at[j], dst_piece, p2_send, p2_recv, (to_x, to_b)).start()
+
+        return carry
+
+    lax.fori_loop(0, n_blk, forward, 0)
 
     group = 4
 
@@ -383,15 +427,17 @@
                 jnp.concatenate([back_full[it, a, rows, :], back_recv[it, rows, :]], axis=0)
             )
         corr[it, :, ch * lanes : (ch + 1) * lanes] = from_left(mxtc[...], jnp.concatenate(parts, axis=1))
-        for copy in corr_copies(it, ch):
-            copy.start()
+        for i, copy in enumerate(corr_copies(it, ch)[:4]):
+            send_along(corr_plan[i][0], copy)
 
     def updated(it, ch):
-        for copy in corr_copies(it, ch):
-            copy.wait_recv()
+        for i, copy in enumerate(corr_copies(it, ch)[2:]):
+            take_along(corr_plan[2 + i][0], copy)
         cols = slice(ch * lanes, (ch + 1) * lanes)
-        total = corr[it, EDGE : EDGE + SUB, cols] + from_m1[it, :, cols] + from_p1[it, :, cols]
-        total = total + jnp.concatenate([from_m2[it, :, cols], from_p2[it, :, cols]], axis=0)
+        total = corr[it, EDGE : EDGE + SUB, cols] + jnp.concatenate([
+            came[it, 4, :, cols] + came[it, 3, :, cols],
+            came[it, 2, :, cols] + came[it, 5, :, cols],
+        ], axis=0)
         return win[it, EDGE : EDGE + SUB, cols] * (total / VIEWS)
 
     def out_cols(ch, core):
@@ -400,12 +446,31 @@
     def out_copies(ch):
         src = out_half.at[:, ch * y_chunk : (ch + 1) * y_chunk, :]
         dst = out_ref.at[rows_here, out_cols(ch, a), :]
-        own = pltpu.make_async_copy(src, dst, o_recv)
+        own = pltpu.make_async_copy(src, dst, o_recv.at[ch, a, 0])
         mates = [
-            remote(src, dst, o_send.at[ch, i], o_recv, (lax.rem(x + i, 4), 2 * c + par))
-            for i in range(4)
+            remote(src, dst, o_send.at[ch, i], o_recv.at[ch, a, min(i, 1)], (to_x, 2 * c + par))
+            for i, to_x in enumerate((x, lax.rem(x + 1, 4), lax.rem(x + 3, 4)))
         ]
         return own, mates
+
+    flip = lax.rem(c, 2)
+    odd = lax.rem(x + 1 - flip, 2)
+    ahead = lax.rem(x - snake(2 * a + odd, c) + 4, 4)
+    onward = lax.rem(x + 2 - ahead + 4, 4)
+    onward_rows = pl.ds(odd * SUB + 8 * (ahead // 2), 8)
+    odd_rows = pl.ds(odd * SUB, SUB)
+
+    def onward_copies(ch):
+        copies = []
+        for h in range(2):
+            part = out_ref.at[onward_rows, out_cols(ch, h), :]
+            copies.append(remote(part, part, f_send.at[ch, h], o_recv.at[ch, h, 0], (onward, b)))
+        return copies
+
+    def send_on(ch):
+        for h, copy in enumerate(onward_copies(ch)):
+            await_bytes(out_ref.at[odd_rows, out_cols(ch, h), :], o_recv.at[ch, h, 1])
+            copy.start()
 
     for it in range(ITERS):
         for ch in range(CHUNKS):
@@ -429,34 +494,47 @@
             back_copy(it, v).wait_recv()
         for ch in range(CHUNKS):
             back_x(it, ch)
-        for ch in range(CHUNKS):
+        def finish(ch):
             new = updated(it, ch)
             if it + 1 < ITERS:
                 win[it + 1, EDGE : EDGE + SUB, ch * lanes : (ch + 1) * lanes] = new
-                for copy in halo_copies(it + 1, ch):
-                    copy.start()
+                for i, copy in enumerate(halo_copies(it + 1, ch)[:4]):
+                    send_along(halo_plan[i][0], copy)
+                return
+            for y in range(y_chunk):
+                out_flat[ch, pl.ds(y, SUB, stride=y_chunk), :] = new[
+                    :, y * z_cells : (y + 1) * z_cells
+                ]
+            out_half[:, ch * y_chunk : (ch + 1) * y_chunk, :] = out_flat[ch].reshape(
+                SUB, y_chunk, z_cells
+            )
+            own, mates = out_copies(ch)
+            for mate in mates[1:]:
+                mate.start()
+
+            @pl.when(a == par)
+            def _():
+                own.start()
+
+            @pl.when(a != par)
+            def _():
+                mates[0].start()
+
+        def move_on(ch):
+            if it + 1 < ITERS:
+                pass_on(it + 1, ch)
             else:
-                for y in range(y_chunk):
-                    out_flat[ch, pl.ds(y, SUB, stride=y_chunk), :] = new[
-                        :, y * z_cells : (y + 1) * z_cells
-                    ]
-                out_half[:, ch * y_chunk : (ch + 1) * y_chunk, :] = out_flat[ch].reshape(
-                    SUB, y_chunk, z_cells
-                )
-                own, mates = out_copies(ch)
-                for mate in mates[1:]:
-                    mate.start()
-
-                @pl.when(a == par)
-                def _():
-                    own.start()
-
-                @pl.when(a != par)
-                def _():
-                    mates[0].start()
-        if it + 1 < ITERS:
-            for ch in range(CHUNKS):
-                blur_x(it + 1, ch)
+                send_on(ch)
+
+        for t in range(CHUNKS + 3):
+            if t < CHUNKS:
+                merge(it, t)
+            if 0 <= t - 1 < CHUNKS:
+                finish(t - 1)
+            if 0 <= t - 2 < CHUNKS:
+                move_on(t - 2)
+            if 0 <= t - 3 < CHUNKS and it + 1 < ITERS:
+                blur_x(it + 1, t - 3)
 
     await_bytes(id_row.at[: row_size - 1], id1_send)
     await_bytes(id_all.at[: n_rows - 1], id2_send)
@@ -475,20 +553,23 @@
         copy.wait_send()
     for it in range(ITERS):
         for ch in range(CHUNKS):
-            for copy in halo_copies(it, ch) + corr_copies(it, ch) + [x_copy(it, ch)]:
-                copy.wait_send()
+            for i in range(6):
+                sent_along(halo_plan[i][0], halo_copies(it, ch)[i])
+                sent_along(corr_plan[i][0], corr_copies(it, ch)[i])
+            x_copy(it, ch).wait_send()
         for v in range(2):
             back_copy(it, v).wait_send()
     for ch in range(CHUNKS):
         own, mates = out_copies(ch)
-        for mate in mates[1:]:
-            mate.wait_send()
+        for copy in mates[1:] + onward_copies(ch):
+            copy.wait_send()
 
         @pl.when(a != par)
         def _():
             mates[0].wait_send()
 
-    await_bytes(out_ref, o_recv)
+        for h in range(2):
+            await_bytes(out_half.at[:, :y_chunk, :], o_recv.at[ch, h, 0])
 
 
 def per_device(estimate, view_data, slot_block, offsets, taps):
@@ -542,20 +623,18 @@
             vmem((ITERS, 2, 2 * SUB * y_half, z_cells), F32),
             vmem((ITERS, 2 * SUB * y_half, z_cells), F32),
             vmem((ITERS, WIN, width), F32),
-            vmem((ITERS, SUB, width), F32),
-            vmem((ITERS, SUB, width), F32),
-            vmem((ITERS, 8, width), F32),
-            vmem((ITERS, 8, width), F32),
+            vmem((ITERS, 6, 8, width), F32),
+            vmem((ITERS, 2, 8, width), F32),
             vmem((CHUNKS, SUB * y_chunk, z_cells), F32),
             vmem((SUB, y_half, z_cells), F32),
             dma, dma, dma, dma, dma,
             dma, dma, dma, dma,
             dma((7,)), dma((7,)), dma, dma,
-            dma((ITERS, CHUNKS, 4)), dma((ITERS, CHUNKS, 4)),
+            dma((ITERS, CHUNKS, 6)), dma((ITERS, CHUNKS, 6)),
             dma((ITERS, CHUNKS)), dma((ITERS, CHUNKS)),
             dma((ITERS, 2)), dma((ITERS, 2)),
-            dma((ITERS, CHUNKS, 4)), dma((ITERS, CHUNKS, 4)),
-            dma((CHUNKS, 4)), dma,
+            dma((ITERS, CHUNKS, 6)), dma((ITERS, CHUNKS, 6)),
+            dma((CHUNKS, 3)), dma((CHUNKS, 2)), dma((CHUNKS, 2, 2)),
             regular, regular,
         ],
         compiler_params=pltpu.CompilerParams(

time: 145 us -> 137 us (0.945)
  Pallas kernels: 141 us -> 133 us
    pallas_call x1, Pallas kernels: 141 us -> 133 us  [per_device(): pl.pallas_call(functools.partial(kernel, n_blk, row_size, y_cells, z_cell...]
where the time goes in v4:
time: 137 us; the launch traced here: 135 us
  Pallas kernels  133 us (97%)
    pallas_call x1, Pallas kernels, per_device(): pl.pallas_call(functools.partial(kernel, n_blk, row_size, y_cells, z_cell...  133 us

profile of v4, /device:TPU:1, one launch (start us, length us, event | category | flops | bytes accessed | tf_op | source)
XLA Modules:
  0.0 135.5 jit_solution(10418469674517433381)
XLA Ops:
  0.7 0.0 copy-start
  1.3 0.0 copy-done
  1.3 133.1 %shard_map.55 = f32[32,64,128]{2,1,0:T(8,128)S(1)} custom-call(s32[1,1]{1,0:T(1,128)S(6)} %copy.8.slot_ref, s32[1,1]{1,0:T(1,128)S(6)} %copy.9.off_ref, f32[1,3,31]{2,1,0:T(4,128)S(1)} %copy.6.taps_ref, f32[32,64,128]{2,1,0:T(8,128)} %est_ref.1, f32[128,16,128]{2,1,0:T(8,128)} %bitcast.1), custom_call_target="tpu_custom_call" | custom-call | tf_op jit(solution)/shard_map/pallas_call | solution.py:589
  134.5 1.0 copy.10
  (1 shorter events, 0.0 us)
Async XLA Ops:
  0.7 0.7 copy-start

commit v5 on v4

--- a/solution.py
+++ b/solution.py
@@ -388,7 +388,7 @@
 
     lax.fori_loop(0, n_blk, forward, 0)
 
-    group = 4
+    group = 8
 
     def blur_yz(it, g):
         v = g // (SUB // group)
@@ -480,7 +480,7 @@
                 blurred[g] = blur_yz(0, g)
                 return carry
 
-            lax.fori_loop(0, 2 * SUB // group, first, 0)
+            lax.fori_loop(0, 2 * SUB // group, first, 0, unroll=2)
             await_bytes(meas, p2_recv)
         per_view = SUB // group
         for v in range(2):
@@ -488,7 +488,7 @@
                 back_yz(it, g, blurred[g] if it == 0 else blur_yz(it, g))
                 return carry
 
-            lax.fori_loop(v * per_view, (v + 1) * per_view, both, 0)
+            lax.fori_loop(v * per_view, (v + 1) * per_view, both, 0, unroll=True)
             back_copy(it, v).start()
         for v in range(2):
             back_copy(it, v).wait_recv()
@@ -619,7 +619,7 @@
             vmem((ITERS, WIN, width), F32),
             vmem((ITERS, 2, CHUNKS, 2 * SUB * y_chunk, z_cells), F32),
             vmem((ITERS, CHUNKS, 2 * SUB * y_chunk, z_cells), F32),
-            vmem((2 * SUB // 4, y_cells, 4 * z_cells), F32),
+            vmem((2 * SUB // 8, y_cells, 8 * z_cells), F32),
             vmem((ITERS, 2, 2 * SUB * y_half, z_cells), F32),
             vmem((ITERS, 2 * SUB * y_half, z_cells), F32),
             vmem((ITERS, WIN, width), F32),

time: 137 us -> 132 us (0.964)
  Pallas kernels: 133 us -> 128 us
    pallas_call x1, Pallas kernels: 133 us -> 128 us  [per_device(): pl.pallas_call(functools.partial(kernel, n_blk, row_size, y_cells, z_cell...]
where the time goes in v5:
time: 132 us; the launch traced here: 131 us
  Pallas kernels  128 us (97%)
  between operations  1.33 us (1%)
    pallas_call x1, Pallas kernels, per_device(): pl.pallas_call(functools.partial(kernel, n_blk, row_size, y_cells, z_cell...  128 us

profile of v5, /device:TPU:1, one launch (start us, length us, event | category | flops | bytes accessed | tf_op | source)
XLA Modules:
  0.0 130.8 jit_solution(4460278529758669308)
XLA Ops:
  0.7 0.0 copy-start
  1.3 0.0 copy-done
  1.3 128.5 %shard_map.55 = f32[32,64,128]{2,1,0:T(8,128)S(1)} custom-call(s32[1,1]{1,0:T(1,128)S(6)} %copy.8.slot_ref, s32[1,1]{1,0:T(1,128)S(6)} %copy.9.off_ref, f32[1,3,31]{2,1,0:T(4,128)S(1)} %copy.6.taps_ref, f32[32,64,128]{2,1,0:T(8,128)} %est_ref.1, f32[128,16,128]{2,1,0:T(8,128)} %bitcast.1), custom_call_target="tpu_custom_call" | custom-call | tf_op jit(solution)/shard_map/pallas_call | solution.py:589
  129.8 1.0 copy.10
  (1 shorter events, 0.0 us)
Async XLA Ops:
  0.7 0.7 copy-start
